TPU v7x, 32 devices: a whole 2x2x4 slice. The times are simulated.
32 devices in a mesh: row: 4 (over x, core), col: 4 (over z), layer: 2 (over y).
Axes of the slice: x: 2, y: 2, z: 4, core: 2. Of those that a mesh axis runs over, the one named last changes fastest.
Arguments:
- interface_panel: float32 [512, 1024], P('col', 'row'), may hold values from -6 to 6
- coupling: float32 [2, 1, 1024, 512], P('layer', None, 'row', 'col'), may hold values from -0.125 to 0.125
- solved_coupling: float32 [2048, 1024], P(('layer', 'col'), 'row'), may hold values from -6 to 6
Outputs:
- schur_panel: float32 [512, 1024], P('col', 'row')
All inputs are finite; a program needn't handle non-finite values.
Results may differ from a plain program's by a relative error of at most 0.00007.
Values sent between devices are 32-bit elements; how exact they have to be, the bound alone decides.
No kernel may reach another device: no remote copies, remote signals or barrier semaphores. Data moves between devices by JAX's collectives and lax.ppermute only.
A program may use at most 64 MiB of HBM per device.

v0:
```python
import jax
import jax.numpy as jnp
from jax import lax
from jax.sharding import PartitionSpec as P


def from_behind(value, axis, steps):
    count = lax.axis_size(axis)
    pairs = [(source, (source + steps) % count) for source in range(count)]
    return lax.ppermute(value, axis, pairs)


def multiply(block, solved):
    return lax.dot_general(
        block,
        solved,
        (((0,), (0,)), ((), ())),
        precision=lax.Precision.HIGHEST,
        preferred_element_type=jnp.float32,
    )


def shards(interface_panel, coupling, solved_coupling):
    blocks = coupling[0]
    rows_here = lax.axis_size("row")
    cols_here = lax.axis_size("col")
    empty = jnp.zeros((blocks.shape[2], solved_coupling.shape[1]), jnp.float32)
    row_id = lax.axis_index("row")
    col_id = lax.axis_index("col")
    for bit in range(cols_here.bit_length() - 1):
        span = 1 << bit
        if span < rows_here:
            moved = from_behind(blocks, "row", -span)
            moved = jnp.where(row_id >= rows_here - span, jnp.roll(moved, -1, axis=0), moved)
        else:
            moved = jnp.roll(blocks, -(span // rows_here), axis=0)
        blocks = jnp.where(col_id // span % 2 == 1, moved, blocks)
    solved = solved_coupling
    for bit in range(rows_here.bit_length() - 1):
        span = 1 << bit
        moved_rows = from_behind(solved, "col", -span)
        solved = jnp.where(row_id // span % 2 == 1, moved_rows, solved)

    def advance(step, carry):
        total, held, current = carry
        total = total + multiply(held[0], current)
        arrived = from_behind(held, "row", -1)
        held = jnp.where(row_id == rows_here - 1, jnp.roll(arrived, -1, axis=0), arrived)
        current = from_behind(current, "col", -1)
        return (total, held, current)

    total, blocks, solved = lax.fori_loop(0, cols_here - 1, advance, (empty, blocks, solved))
    total = total + multiply(blocks[0], solved)
    summed = lax.psum(total, "layer")
    return interface_panel - summed


def solution(mesh):
    return jax.shard_map(
        shards,
        mesh=mesh,
        in_specs=(P("col", "row"), P("layer", None, "row", "col"), P(("layer", "col"), "row")),
        out_specs=P("col", "row"),
        check_vma=False,
    )
```

profile of v0, /device:TPU:1, one launch (start us, length us, event | category | flops | bytes accessed | tf_op | source)
XLA Modules:
  0.0 90.4 jit_solution(12344220018030673675)
XLA Ops:
  6.5 0.0 all-reduce.2.cloned.1.call-start
  6.5 0.1 collective-permute-start.2
  6.6 4.8 %collective-permute-start.4 = (f32[256,256]{1,0:T(8,128)}, f32[256,256]{1,0:T(8,128)S(1)}, u32[]{:S(2)}, u32[]{:S(2)}) collective-permute-start(f32[256,256]{1,0:T(8,128)} %param.7), channel_id=1, source_target_pairs={{0,6},{2,0},{4,2},{6,4},{1,7},{3,1},{5,3},{7,5},{8,14},{10,8},{12,... | collective-permute-start | bytes 786440 | tf_op jit(solution)/shard_map/ppermute | solution.py:10
  11.4 0.6 collective-permute-done.2
  12.0 0.9 %broadcast_select_fusion.2 = f32[1,256,128]{2,1,0:T(8,128)S(1)} fusion(f32[1,256,128]{2,1,0:T(8,128)S(1)} %collective-permute-done.2, pred[]{:T(512)S(6)} %eq.19, f32[1,1,256,128]{3,2,1,0:T(8,128)} %param.6), kind=kLoop, calls=%fused_computation.6 | loop fusion | flops 32768 | bytes 393217 | tf_op jit(solution)/shard_map/jit(_where)/select_n | solution.py:37
  12.9 1.5 %collective-permute-start.3 = (f32[1,256,128]{2,1,0:T(8,128)S(1)}, f32[1,256,128]{2,1,0:T(8,128)S(1)}, u32[]{:S(2)}, u32[]{:S(2)}) collective-permute-start(f32[1,256,128]{2,1,0:T(8,128)S(1)} %broadcast_select_fusion.2), channel_id=1, source_target_pairs={{0,16},{8,24},{16,0},{24,8},{1,17},{9,25},{17,1},{25,9},{2,18},{10... | collective-permute-start | bytes 393224 | tf_op jit(solution)/shard_map/ppermute | solution.py:10
  14.5 1.9 %collective-permute-done.4 = f32[256,256]{1,0:T(8,128)S(1)} collective-permute-done((f32[256,256]{1,0:T(8,128)}, f32[256,256]{1,0:T(8,128)S(1)}, u32[]{:S(2)}, u32[]{:S(2)}) %collective-permute-start.4) | collective-permute-done | bytes 262176 | tf_op jit(solution)/shard_map/ppermute | solution.py:10
  16.4 0.0 copy-done
  16.4 1.1 %collective-permute-start.5 = (f32[256,256]{1,0:T(8,128)S(1)}, f32[256,256]{1,0:T(8,128)S(1)}, u32[]{:S(2)}, u32[]{:S(2)}) collective-permute-start(f32[256,256]{1,0:T(8,128)S(1)} %broadcast_select_fusion), channel_id=1, source_target_pairs={{0,4},{2,6},{4,0},{6,2},{1,5},{3,7},{5,1},{7,3},{8,12},{10,14},{12... | collective-permute-start | bytes 786440 | tf_op jit(solution)/shard_map/ppermute | solution.py:10
  17.5 0.2 collective-permute-done.3
  17.7 11.9 %collective-permute-done.5 = f32[256,256]{1,0:T(8,128)S(1)} collective-permute-done((f32[256,256]{1,0:T(8,128)S(1)}, f32[256,256]{1,0:T(8,128)S(1)}, u32[]{:S(2)}, u32[]{:S(2)}) %collective-permute-start.5) | collective-permute-done | bytes 262176 | tf_op jit(solution)/shard_map/ppermute | solution.py:10
  29.6 28.7 %while.16 = (s32[]{:T(128)}, f32[128,256]{1,0:T(8,128)S(1)}, f32[1,256,128]{2,1,0:T(8,128)S(1)}, f32[256,256]{1,0:T(8,128)S(1)}, s32[]{:T(128)}, /*index=5*/s32[]{:T(128)}) while((s32[]{:T(128)}, f32[128,256]{1,0:T(8,128)S(1)}, f32[1,256,128]{2,1,0:T(8,128)S(1)}, f32[256,256]{1,0:T(8,128)S(1)}, s32[]{:T(128)}, ...), condition=%wide.region_1.2_spmd.clone, body=%wide.region_0.1_spmd.clone.sunk | while | flops 100728832 | bytes 3014815 | solution.py:52
  29.7 3.6 %collective-permute-start.1 = (f32[256,256]{1,0:T(8,128)S(1)}, f32[256,256]{1,0:T(8,128)S(1)}, u32[]{:S(2)}, u32[]{:S(2)}) collective-permute-start(f32[256,256]{1,0:T(8,128)S(1)} %copy.11), channel_id=1, source_target_pairs={{0,6},{2,0},{4,2},{6,4},{1,7},{3,1},{5,3},{7,5},{8,14},{10,8},{12,... | collective-permute-start | bytes 786440 | tf_op jit(solution)/shard_map/while/body/eval_jaxpr/ppermute | solution.py:10
  33.3 0.8 collective-permute-start
  34.2 0.4 convolution_add_fusion.2
  34.6 4.4 %collective-permute-done = f32[1,256,128]{2,1,0:T(8,128)S(1)} collective-permute-done((f32[1,256,128]{2,1,0:T(8,128)S(1)}, f32[1,256,128]{2,1,0:T(8,128)S(1)}, u32[]{:S(2)}, u32[]{:S(2)}) %collective-permute-start) | collective-permute-done | bytes 131104 | tf_op jit(solution)/shard_map/while/body/eval_jaxpr/ppermute | solution.py:10
  39.0 0.0 collective-permute-done.1
  39.0 3.6 %collective-permute-start.1 = (f32[256,256]{1,0:T(8,128)S(1)}, f32[256,256]{1,0:T(8,128)S(1)}, u32[]{:S(2)}, u32[]{:S(2)}) collective-permute-start(f32[256,256]{1,0:T(8,128)S(1)} %copy.11), channel_id=1, source_target_pairs={{0,6},{2,0},{4,2},{6,4},{1,7},{3,1},{5,3},{7,5},{8,14},{10,8},{12,... | collective-permute-start | bytes 786440 | tf_op jit(solution)/shard_map/while/body/eval_jaxpr/ppermute | solution.py:10
  42.6 1.7 %collective-permute-start = (f32[1,256,128]{2,1,0:T(8,128)S(1)}, f32[1,256,128]{2,1,0:T(8,128)S(1)}, u32[]{:S(2)}, u32[]{:S(2)}) collective-permute-start(f32[1,256,128]{2,1,0:T(8,128)S(1)} %copy.10), channel_id=1, source_target_pairs={{0,24},{8,0},{16,8},{24,16},{1,25},{9,1},{17,9},{25,17},{2,26},{10... | collective-permute-start | bytes 393224 | tf_op jit(solution)/shard_map/while/body/eval_jaxpr/ppermute | solution.py:10
  44.3 0.4 convolution_add_fusion.2
  44.7 4.4 %collective-permute-done = f32[1,256,128]{2,1,0:T(8,128)S(1)} collective-permute-done((f32[1,256,128]{2,1,0:T(8,128)S(1)}, f32[1,256,128]{2,1,0:T(8,128)S(1)}, u32[]{:S(2)}, u32[]{:S(2)}) %collective-permute-start) | collective-permute-done | bytes 131104 | tf_op jit(solution)/shard_map/while/body/eval_jaxpr/ppermute | solution.py:10
  49.1 0.0 collective-permute-done.1
  49.1 1.8 %collective-permute-start.1 = (f32[256,256]{1,0:T(8,128)S(1)}, f32[256,256]{1,0:T(8,128)S(1)}, u32[]{:S(2)}, u32[]{:S(2)}) collective-permute-start(f32[256,256]{1,0:T(8,128)S(1)} %copy.11), channel_id=1, source_target_pairs={{0,6},{2,0},{4,2},{6,4},{1,7},{3,1},{5,3},{7,5},{8,14},{10,8},{12,... | collective-permute-start | bytes 786440 | tf_op jit(solution)/shard_map/while/body/eval_jaxpr/ppermute | solution.py:10
  50.9 2.6 %collective-permute-start = (f32[1,256,128]{2,1,0:T(8,128)S(1)}, f32[1,256,128]{2,1,0:T(8,128)S(1)}, u32[]{:S(2)}, u32[]{:S(2)}) collective-permute-start(f32[1,256,128]{2,1,0:T(8,128)S(1)} %copy.10), channel_id=1, source_target_pairs={{0,24},{8,0},{16,8},{24,16},{1,25},{9,1},{17,9},{25,17},{2,26},{10... | collective-permute-start | bytes 393224 | tf_op jit(solution)/shard_map/while/body/eval_jaxpr/ppermute | solution.py:10
  53.5 0.4 convolution_add_fusion.2
  53.9 4.4 %collective-permute-done = f32[1,256,128]{2,1,0:T(8,128)S(1)} collective-permute-done((f32[1,256,128]{2,1,0:T(8,128)S(1)}, f32[1,256,128]{2,1,0:T(8,128)S(1)}, u32[]{:S(2)}, u32[]{:S(2)}) %collective-permute-start) | collective-permute-done | bytes 131104 | tf_op jit(solution)/shard_map/while/body/eval_jaxpr/ppermute | solution.py:10
  58.3 0.0 collective-permute-done.1
  58.3 0.4 fusion.1
  58.7 0.7 add.34
  59.4 0.0 all-reduce.2.cloned.1.call-update
  59.4 22.6 %all-reduce.2.cloned.1.call-done = f32[128,256]{1,0:T(8,128)} async-done(((f32[128,256]{1,0:T(8,128)}), f32[128,256]{1,0:T(8,128)}) %all-reduce.2.cloned.1.call-update) | async-done | bytes 131088 | tf_op jit(solution)/shard_map/psum | solution.py:54
  82.0 1.6 %sub.14 = f32[128,256]{1,0:T(8,128)} subtract(f32[128,256]{1,0:T(8,128)S(1)} %copy-done.1, f32[128,256]{1,0:T(8,128)} %all-reduce.2.cloned.1.call-done) | non-fusion elementwise | flops 32768 | bytes 393216 | tf_op jit(solution)/shard_map/sub | solution.py:55
  (13 shorter events, 0.2 us)
Async XLA Ops:
  6.5 9.8 %copy-start = (f32[256,256]{1,0:T(8,128)S(1)}, f32[256,256]{1,0:T(8,128)}, u32[]{:S(2)}) copy-start(f32[256,256]{1,0:T(8,128)} %param.7) | copy-start | bytes 786436
  6.5 75.5 %all-reduce.2.cloned.1.call-start = ((), (), s32[]{:S(2)}) async-start(), calls=%async_computation | async-start | bytes 262144 | tf_op jit(solution)/shard_map/psum | solution.py:54
  6.5 5.5 %collective-permute-start.2 = (f32[1,256,128]{2,1,0:T(8,128)}, f32[1,256,128]{2,1,0:T(8,128)S(1)}, u32[]{:S(2)}, u32[]{:S(2)}) collective-permute-start(f32[1,256,128]{2,1,0:T(8,128)} %bitcast.14), channel_id=1, source_target_pairs={{0,24},{8,0},{16,8},{24,16},{1,25},{9,1},{17,9},{25,17},{2,26},{10... | collective-permute-start | bytes 393224 | tf_op jit(solution)/shard_map/ppermute | solution.py:10
  6.6 9.8 %collective-permute-start.4 = (f32[256,256]{1,0:T(8,128)}, f32[256,256]{1,0:T(8,128)S(1)}, u32[]{:S(2)}, u32[]{:S(2)}) collective-permute-start(f32[256,256]{1,0:T(8,128)} %param.7), channel_id=1, source_target_pairs={{0,6},{2,0},{4,2},{6,4},{1,7},{3,1},{5,3},{7,5},{8,14},{10,8},{12,... | collective-permute-start | bytes 786440 | tf_op jit(solution)/shard_map/ppermute | solution.py:10
  12.9 4.8 %collective-permute-start.3 = (f32[1,256,128]{2,1,0:T(8,128)S(1)}, f32[1,256,128]{2,1,0:T(8,128)S(1)}, u32[]{:S(2)}, u32[]{:S(2)}) collective-permute-start(f32[1,256,128]{2,1,0:T(8,128)S(1)} %broadcast_select_fusion.2), channel_id=1, source_target_pairs={{0,16},{8,24},{16,0},{24,8},{1,17},{9,25},{17,1},{25,9},{2,18},{10... | collective-permute-start | bytes 393224 | tf_op jit(solution)/shard_map/ppermute | solution.py:10
  16.4 13.2 %collective-permute-start.5 = (f32[256,256]{1,0:T(8,128)S(1)}, f32[256,256]{1,0:T(8,128)S(1)}, u32[]{:S(2)}, u32[]{:S(2)}) collective-permute-start(f32[256,256]{1,0:T(8,128)S(1)} %broadcast_select_fusion), channel_id=1, source_target_pairs={{0,4},{2,6},{4,0},{6,2},{1,5},{3,7},{5,1},{7,3},{8,12},{10,14},{12... | collective-permute-start | bytes 786440 | tf_op jit(solution)/shard_map/ppermute | solution.py:10
  29.7 9.3 %collective-permute-start.1 = (f32[256,256]{1,0:T(8,128)S(1)}, f32[256,256]{1,0:T(8,128)S(1)}, u32[]{:S(2)}, u32[]{:S(2)}) collective-permute-start(f32[256,256]{1,0:T(8,128)S(1)} %copy.11), channel_id=1, source_target_pairs={{0,6},{2,0},{4,2},{6,4},{1,7},{3,1},{5,3},{7,5},{8,14},{10,8},{12,... | collective-permute-start | bytes 786440 | tf_op jit(solution)/shard_map/while/body/eval_jaxpr/ppermute | solution.py:10
  33.3 5.6 %collective-permute-start = (f32[1,256,128]{2,1,0:T(8,128)S(1)}, f32[1,256,128]{2,1,0:T(8,128)S(1)}, u32[]{:S(2)}, u32[]{:S(2)}) collective-permute-start(f32[1,256,128]{2,1,0:T(8,128)S(1)} %copy.10), channel_id=1, source_target_pairs={{0,24},{8,0},{16,8},{24,16},{1,25},{9,1},{17,9},{25,17},{2,26},{10... | collective-permute-start | bytes 393224 | tf_op jit(solution)/shard_map/while/body/eval_jaxpr/ppermute | solution.py:10
  39.0 10.1 %collective-permute-start.1 = (f32[256,256]{1,0:T(8,128)S(1)}, f32[256,256]{1,0:T(8,128)S(1)}, u32[]{:S(2)}, u32[]{:S(2)}) collective-permute-start(f32[256,256]{1,0:T(8,128)S(1)} %copy.11), channel_id=1, source_target_pairs={{0,6},{2,0},{4,2},{6,4},{1,7},{3,1},{5,3},{7,5},{8,14},{10,8},{12,... | collective-permute-start | bytes 786440 | tf_op jit(solution)/shard_map/while/body/eval_jaxpr/ppermute | solution.py:10
  42.6 6.5 %collective-permute-start = (f32[1,256,128]{2,1,0:T(8,128)S(1)}, f32[1,256,128]{2,1,0:T(8,128)S(1)}, u32[]{:S(2)}, u32[]{:S(2)}) collective-permute-start(f32[1,256,128]{2,1,0:T(8,128)S(1)} %copy.10), channel_id=1, source_target_pairs={{0,24},{8,0},{16,8},{24,16},{1,25},{9,1},{17,9},{25,17},{2,26},{10... | collective-permute-start | bytes 393224 | tf_op jit(solution)/shard_map/while/body/eval_jaxpr/ppermute | solution.py:10
  49.1 9.2 %collective-permute-start.1 = (f32[256,256]{1,0:T(8,128)S(1)}, f32[256,256]{1,0:T(8,128)S(1)}, u32[]{:S(2)}, u32[]{:S(2)}) collective-permute-start(f32[256,256]{1,0:T(8,128)S(1)} %copy.11), channel_id=1, source_target_pairs={{0,6},{2,0},{4,2},{6,4},{1,7},{3,1},{5,3},{7,5},{8,14},{10,8},{12,... | collective-permute-start | bytes 786440 | tf_op jit(solution)/shard_map/while/body/eval_jaxpr/ppermute | solution.py:10
  50.9 7.4 %collective-permute-start = (f32[1,256,128]{2,1,0:T(8,128)S(1)}, f32[1,256,128]{2,1,0:T(8,128)S(1)}, u32[]{:S(2)}, u32[]{:S(2)}) collective-permute-start(f32[1,256,128]{2,1,0:T(8,128)S(1)} %copy.10), channel_id=1, source_target_pairs={{0,24},{8,0},{16,8},{24,16},{1,25},{9,1},{17,9},{25,17},{2,26},{10... | collective-permute-start | bytes 393224 | tf_op jit(solution)/shard_map/while/body/eval_jaxpr/ppermute | solution.py:10
  59.4 22.6 %copy-start.1 = (f32[128,256]{1,0:T(8,128)S(1)}, f32[128,256]{1,0:T(8,128)}, u32[]{:S(2)}) copy-start(f32[128,256]{1,0:T(8,128)} %param.5) | copy-start | bytes 393220
Sparse Core Ops, SparseCore 0:
  59.5 22.3 all-reduce.1
where the time goes:
time: 91.6 us; the launch traced here: 90.4 us
  waiting for transfers between devices  50.3 us (55%)
  starting transfers between devices  21.6 us (24%)
  between operations  13.4 us (15%)
  other arithmetic  3.25 us (4%)
  matrix products  1.63 us (2%)
    ppermute x10, waiting for transfers between devices, from_behind(): return lax.ppermute(value, axis, pairs)  27.7 us
    psum x1, waiting for transfers between devices, shards(): summed = lax.psum(total, 'layer')  22.6 us
    ppermute x10, starting transfers between devices, from_behind(): return lax.ppermute(value, axis, pairs)  21.6 us
  transfers between devices with their start and end apart: 11, of which 8 were waited for; matrix products, arithmetic and copies ran while one was open for 2% of the time, Pallas kernels for 0%

commit v1 on v0

--- a/solution.py
+++ b/solution.py
@@ -2,6 +2,18 @@
 import jax.numpy as jnp
 from jax import lax
 from jax.sharding import PartitionSpec as P
+
+MESH_AXES = ("row", "col", "layer")
+
+
+def multiply(block, solved):
+    return lax.dot_general(
+        block,
+        solved,
+        (((0,), (0,)), ((), ())),
+        precision=lax.Precision.HIGH,
+        preferred_element_type=jnp.float32,
+    )
 
 
 def from_behind(value, axis, steps):
@@ -10,17 +22,7 @@
     return lax.ppermute(value, axis, pairs)
 
 
-def multiply(block, solved):
-    return lax.dot_general(
-        block,
-        solved,
-        (((0,), (0,)), ((), ())),
-        precision=lax.Precision.HIGHEST,
-        preferred_element_type=jnp.float32,
-    )
-
-
-def shards(interface_panel, coupling, solved_coupling):
+def ring(interface_panel, coupling, solved_coupling):
     blocks = coupling[0]
     rows_here = lax.axis_size("row")
     cols_here = lax.axis_size("col")
@@ -51,11 +53,67 @@
 
     total, blocks, solved = lax.fori_loop(0, cols_here - 1, advance, (empty, blocks, solved))
     total = total + multiply(blocks[0], solved)
-    summed = lax.psum(total, "layer")
-    return interface_panel - summed
+    for step in range(1, lax.axis_size("layer")):
+        interface_panel = interface_panel - from_behind(total, "layer", step)
+    return interface_panel - total
+
+
+def is_home(r, c):
+    return (r ^ c) & 1 == 0
+
+
+def route(target):
+    pairs = []
+    for r in range(4):
+        for c in range(4):
+            for l in range(2):
+                to = target(r, c, l)
+                if to is not None:
+                    pairs.append((r * 8 + c * 2 + l, to[0] * 8 + to[1] * 2 + to[2]))
+    return pairs
+
+
+def pairs_of_planes(interface_panel, coupling, solved):
+    def send(value, target):
+        return lax.ppermute(value, MESH_AXES, route(target))
+
+    b = coupling[0, 0]
+    r = lax.axis_index("row")
+    c = lax.axis_index("col")
+    home = is_home(r, c)
+    aligned = r // 2 == c // 2
+    far = send(solved, lambda r, c, l: (r, c ^ 2, l) if is_home(r, c) else (r ^ 1, c ^ 3, l))
+    near = send(solved, lambda r, c, l: None if is_home(r, c) else (r ^ 1, c ^ 1, l))
+    b_z = send(b, lambda r, c, l: (r, c ^ 1, l))
+    b_x = send(b, lambda r, c, l: (r ^ 2, c, l))
+    b_zx = send(b_z, lambda r, c, l: (r ^ 2, c, l))
+    far, near, b_z, b_x, b_zx = lax.optimization_barrier((far, near, b_z, b_x, b_zx))
+    here = jnp.where(home, solved, near)
+
+    def both(own, other):
+        return jnp.concatenate([jnp.where(home, other, own), jnp.where(home, own, other)], 1)
+
+    block_here = both(jnp.where(aligned, b, b_x), jnp.where(aligned, b_z, b_zx))
+    block_far = both(jnp.where(aligned, b_x, b), jnp.where(aligned, b_zx, b_z))
+    early = multiply(block_here, here)
+    early, far = lax.optimization_barrier((early, far))
+    total = early + multiply(block_far, far)
+    rows = b.shape[1]
+    part = total[:rows] + send(total[rows:], lambda r, c, l: (r ^ 1, c, l))
+    to_owner = lambda r, c, l: (r, c ^ 1, l) if is_home(r, c) else (r ^ 1, c, l)
+    one = send(part, to_owner)
+    two = send(part, lambda r, c, l: to_owner(r, c, l)[:2] + (1 - l,))
+    return interface_panel - one - two
 
 
 def solution(mesh):
+    small = tuple(mesh.shape[axis] for axis in MESH_AXES) == (4, 4, 2)
+
+    def shards(interface_panel, coupling, solved_coupling):
+        if small and coupling.shape[1] == 1 and coupling.shape[2] == solved_coupling.shape[0]:
+            return pairs_of_planes(interface_panel, coupling, solved_coupling)
+        return ring(interface_panel, coupling, solved_coupling)
+
     return jax.shard_map(
         shards,
         mesh=mesh,

time: 91.6 us -> 28 us (0.31); the launches traced: 90.4 us -> 27.9 us
  waiting for transfers between devices: 50.3 us -> 15.3 us
  between operations: 13.4 us -> 0.07 us
  starting transfers between devices: 21.6 us -> 10 us
  other arithmetic: 3.25 us -> 1.65 us
    psum x1 -> x0, waiting for transfers between devices: 22.6 us -> none  [shards(): summed = lax.psum(total, 'layer')]
    ppermute x10 -> x8, waiting for transfers between devices: 27.7 us -> 15.3 us  [send(): return lax.ppermute(value, MESH_AXES, route(target))]
    ppermute x10 -> x8, starting transfers between devices: 21.6 us -> 10 us  [send(): return lax.ppermute(value, MESH_AXES, route(target))]
  transfers between devices with their start and end apart: 11 -> 8, of which waited for: 8 -> 6; matrix products, arithmetic and copies ran while one was open for 2% -> 0% of each run, Pallas kernels for 0% -> 0%
where the time goes in v1:
time: 28 us; the launch traced here: 27.9 us
  waiting for transfers between devices  15.3 us (55%)
  starting transfers between devices  10 us (36%)
  other arithmetic  1.65 us (6%)
  matrix products  0.79 us (3%)
    ppermute x8, waiting for transfers between devices, send(): return lax.ppermute(value, MESH_AXES, route(target))  15.3 us
    ppermute x8, starting transfers between devices, send(): return lax.ppermute(value, MESH_AXES, route(target))  10 us
    select_n x1, other arithmetic, both(): jnp.where(home, other, own)  0.95 us
    dot_general x2, matrix products, multiply(): lax.dot_general(block, solved, (((0,), (0,)), ((), ())), precision=lax.Pr...  0.79 us
    sub x1, other arithmetic, pairs_of_planes(): return interface_panel - one - two  0.68 us
  transfers between devices with their start and end apart: 8, of which 6 were waited for; matrix products, arithmetic and copies ran while one was open for 0% of the time, Pallas kernels for 0%

profile of v1, /device:TPU:1, one launch (start us, length us, event | category | flops | bytes accessed | tf_op | source)
XLA Modules:
  0.0 27.9 jit_solution(15239768617754477676)
XLA Ops:
  0.0 2.1 %collective-permute-start.2 = (f32[256,128]{1,0:T(8,128)}, f32[256,128]{1,0:T(8,128)S(1)}, u32[]{:S(2)}, u32[]{:S(2)}) collective-permute-start(f32[256,128]{1,0:T(8,128)} %bitcast.6), channel_id=1, source_target_pairs={{0,2},{1,3},{2,0},{3,1},{4,6},{5,7},{6,4},{7,5},{8,10},{9,11},{10,... | collective-permute-start | bytes 393224 | tf_op jit(solution)/shard_map/ppermute | solution.py:78
  2.1 3.0 %collective-permute-start = (f32[256,256]{1,0:T(8,128)}, f32[256,256]{1,0:T(8,128)S(1)}, u32[]{:S(2)}, u32[]{:S(2)}) collective-permute-start(f32[256,256]{1,0:T(8,128)} %param.5), channel_id=1, source_target_pairs={{0,4},{1,5},{2,12},{3,13},{4,0},{5,1},{6,8},{7,9},{8,6},{9,7},{10,... | collective-permute-start | bytes 786440 | tf_op jit(solution)/shard_map/ppermute | solution.py:78
  5.2 1.9 %collective-permute-start.1 = (f32[256,256]{1,0:T(8,128)}, f32[256,256]{1,0:T(8,128)S(1)}, u32[]{:S(2)}, u32[]{:S(2)}) collective-permute-start(f32[256,256]{1,0:T(8,128)} %param.5), channel_id=1, source_target_pairs={{2,8},{3,9},{6,12},{7,13},{8,2},{9,3},{12,6},{13,7},{18,24},{19,25... | collective-permute-start | bytes 786440 | tf_op jit(solution)/shard_map/ppermute | solution.py:78
  7.1 1.3 %collective-permute-start.3 = (f32[256,128]{1,0:T(8,128)}, f32[256,128]{1,0:T(8,128)S(1)}, u32[]{:S(2)}, u32[]{:S(2)}) collective-permute-start(f32[256,128]{1,0:T(8,128)} %bitcast.7), channel_id=1, source_target_pairs={{0,16},{1,17},{2,18},{3,19},{4,20},{5,21},{6,22},{7,23},{8,24},{9,... | collective-permute-start | bytes 393224 | tf_op jit(solution)/shard_map/ppermute | solution.py:78
  8.4 0.0 collective-permute-done.2
  8.4 0.3 collective-permute-start.4
  8.6 0.0 copy-start
  8.6 4.3 %collective-permute-done.3 = f32[256,128]{1,0:T(8,128)S(1)} collective-permute-done((f32[256,128]{1,0:T(8,128)}, f32[256,128]{1,0:T(8,128)S(1)}, u32[]{:S(2)}, u32[]{:S(2)}) %collective-permute-start.3) | collective-permute-done | bytes 131104 | tf_op jit(solution)/shard_map/ppermute | solution.py:78
  12.9 2.5 %collective-permute-done.4 = f32[256,128]{1,0:T(8,128)S(1)} collective-permute-done((f32[256,128]{1,0:T(8,128)S(1)}, f32[256,128]{1,0:T(8,128)S(1)}, u32[]{:S(2)}, u32[]{:S(2)}) %collective-permute-start.4) | collective-permute-done | bytes 131104 | tf_op jit(solution)/shard_map/ppermute | solution.py:78
  15.4 0.0 collective-permute-done
  15.4 2.3 %collective-permute-done.1 = f32[256,256]{1,0:T(8,128)S(1)} collective-permute-done((f32[256,256]{1,0:T(8,128)}, f32[256,256]{1,0:T(8,128)S(1)}, u32[]{:S(2)}, u32[]{:S(2)}) %collective-permute-start.1) | collective-permute-done | bytes 262176 | tf_op jit(solution)/shard_map/ppermute | solution.py:78
  17.7 0.9 %broadcast_select_fusion.5 = (f32[256,128]{1,0:T(8,128)S(1)}, f32[256,128]{1,0:T(8,128)S(1)}, f32[256,128]{1,0:T(8,128)S(1)}, f32[256,128]{1,0:T(8,128)S(1)}) fusion(pred[]{:T(512)S(6)} %eq.6, f32[256,128]{1,0:T(8,128)S(1)} %collective-permute-done.4, f32[256,128]{1,0:T(8,128)S(1)} %collective-permute-done.2, pred[]{:T(512)S(6)} %eq.7, ...), kind=kLoop, calls=%fused_computation.17 | loop fusion | flops 262144 | bytes 1048578 | tf_op jit(solution)/shard_map/jit(_where)/select_n | solution.py:94
  18.6 0.0 copy-done
  18.7 0.4 %fusion = f32[256,256]{1,0:T(8,128)S(1)} fusion(f32[256,128]{1,0:T(8,128)S(1)} %get-tuple-element.20, f32[256,128]{1,0:T(8,128)S(1)} %get-tuple-element.22, f32[256,256]{1,0:T(8,128)S(1)} %copy-done, f32[256,256]{1,0:T(8,128)S(1)} %collective-permute-done.1, pred[]{:T(512)S(6)} %eq.6), kind=kOutput, calls=%fused_computation.1 | convolution fusion | flops 100794368 | bytes 1048577 | tf_op jit(solution)/shard_map/dot_general | solution.py:10
  19.1 0.4 %convolution_add_fusion = f32[256,256]{1,0:T(8,128)S(1)} fusion(f32[256,256]{1,0:T(8,128)S(1)} %fusion, f32[256,256]{1,0:T(8,128)S(1)} %collective-permute-done, f32[256,128]{1,0:T(8,128)S(1)} %get-tuple-element.21, f32[256,128]{1,0:T(8,128)S(1)} %get-tuple-element.19), kind=kOutput, calls=%fused_computation | convolution fusion | flops 100794368 | bytes 1048576 | tf_op jit(solution)/shard_map/dot_general | solution.py:10
  19.5 0.0 copy-start.1
  19.5 0.1 collective-permute-start.5
  19.6 1.3 %collective-permute-done.5 = f32[128,256]{1,0:T(8,128)S(1)} collective-permute-done((f32[128,256]{1,0:T(8,128)S(1)}, f32[128,256]{1,0:T(8,128)S(1)}, u32[]{:S(2)}, u32[]{:S(2)}) %collective-permute-start.5) | collective-permute-done | bytes 131104 | tf_op jit(solution)/shard_map/ppermute | solution.py:78
  20.9 1.3 %collective-permute-start.7 = (f32[128,256]{1,0:T(8,128)S(1)}, f32[128,256]{1,0:T(8,128)S(1)}, u32[]{:S(2)}, u32[]{:S(2)}) collective-permute-start(f32[128,256]{1,0:T(8,128)S(1)} %slice_add_fusion), channel_id=1, source_target_pairs={{0,3},{1,2},{2,11},{3,10},{4,7},{5,6},{6,15},{7,14},{8,1},{9,0},{1... | collective-permute-start | bytes 393224 | tf_op jit(solution)/shard_map/ppermute | solution.py:78
  22.3 0.0 collective-permute-start.6
  22.3 3.5 %collective-permute-done.7 = f32[128,256]{1,0:T(8,128)S(1)} collective-permute-done((f32[128,256]{1,0:T(8,128)S(1)}, f32[128,256]{1,0:T(8,128)S(1)}, u32[]{:S(2)}, u32[]{:S(2)}) %collective-permute-start.7) | collective-permute-done | bytes 131104 | tf_op jit(solution)/shard_map/ppermute | solution.py:78
  25.8 1.4 %collective-permute-done.6 = f32[128,256]{1,0:T(8,128)S(1)} collective-permute-done((f32[128,256]{1,0:T(8,128)S(1)}, f32[128,256]{1,0:T(8,128)S(1)}, u32[]{:S(2)}, u32[]{:S(2)}) %collective-permute-start.6) | collective-permute-done | bytes 131104 | tf_op jit(solution)/shard_map/ppermute | solution.py:78
  27.2 0.0 copy-done.1
  27.2 0.7 %subtract_subtract_fusion = f32[128,256]{1,0:T(8,128)} fusion(f32[128,256]{1,0:T(8,128)S(1)} %collective-permute-done.7, f32[128,256]{1,0:T(8,128)S(1)} %copy-done.1, f32[128,256]{1,0:T(8,128)S(1)} %collective-permute-done.6), kind=kLoop, calls=%fused_computation.10 | loop fusion | flops 65536 | bytes 524288 | tf_op jit(solution)/shard_map/sub | solution.py:106
  (2 shorter events, 0.0 us)
Async XLA Ops:
  0.0 8.4 %collective-permute-start.2 = (f32[256,128]{1,0:T(8,128)}, f32[256,128]{1,0:T(8,128)S(1)}, u32[]{:S(2)}, u32[]{:S(2)}) collective-permute-start(f32[256,128]{1,0:T(8,128)} %bitcast.6), channel_id=1, source_target_pairs={{0,2},{1,3},{2,0},{3,1},{4,6},{5,7},{6,4},{7,5},{8,10},{9,11},{10,... | collective-permute-start | bytes 393224 | tf_op jit(solution)/shard_map/ppermute | solution.py:78
  2.1 13.3 %collective-permute-start = (f32[256,256]{1,0:T(8,128)}, f32[256,256]{1,0:T(8,128)S(1)}, u32[]{:S(2)}, u32[]{:S(2)}) collective-permute-start(f32[256,256]{1,0:T(8,128)} %param.5), channel_id=1, source_target_pairs={{0,4},{1,5},{2,12},{3,13},{4,0},{5,1},{6,8},{7,9},{8,6},{9,7},{10,... | collective-permute-start | bytes 786440 | tf_op jit(solution)/shard_map/ppermute | solution.py:78
  5.2 12.5 %collective-permute-start.1 = (f32[256,256]{1,0:T(8,128)}, f32[256,256]{1,0:T(8,128)S(1)}, u32[]{:S(2)}, u32[]{:S(2)}) collective-permute-start(f32[256,256]{1,0:T(8,128)} %param.5), channel_id=1, source_target_pairs={{2,8},{3,9},{6,12},{7,13},{8,2},{9,3},{12,6},{13,7},{18,24},{19,25... | collective-permute-start | bytes 786440 | tf_op jit(solution)/shard_map/ppermute | solution.py:78
  7.1 5.8 %collective-permute-start.3 = (f32[256,128]{1,0:T(8,128)}, f32[256,128]{1,0:T(8,128)S(1)}, u32[]{:S(2)}, u32[]{:S(2)}) collective-permute-start(f32[256,128]{1,0:T(8,128)} %bitcast.7), channel_id=1, source_target_pairs={{0,16},{1,17},{2,18},{3,19},{4,20},{5,21},{6,22},{7,23},{8,24},{9,... | collective-permute-start | bytes 393224 | tf_op jit(solution)/shard_map/ppermute | solution.py:78
  8.4 7.0 %collective-permute-start.4 = (f32[256,128]{1,0:T(8,128)S(1)}, f32[256,128]{1,0:T(8,128)S(1)}, u32[]{:S(2)}, u32[]{:S(2)}) collective-permute-start(f32[256,128]{1,0:T(8,128)S(1)} %collective-permute-done.2), channel_id=1, source_target_pairs={{0,16},{1,17},{2,18},{3,19},{4,20},{5,21},{6,22},{7,23},{8,24},{9,... | collective-permute-start | bytes 393224 | tf_op jit(solution)/shard_map/ppermute | solution.py:78
  8.6 10.0 %copy-start = (f32[256,256]{1,0:T(8,128)S(1)}, f32[256,256]{1,0:T(8,128)}, u32[]{:S(2)}) copy-start(f32[256,256]{1,0:T(8,128)} %param.5) | copy-start | bytes 786436
  19.5 7.7 %copy-start.1 = (f32[128,256]{1,0:T(8,128)S(1)}, f32[128,256]{1,0:T(8,128)}, u32[]{:S(2)}) copy-start(f32[128,256]{1,0:T(8,128)} %param.3) | copy-start | bytes 393220
  19.5 1.4 %collective-permute-start.5 = (f32[128,256]{1,0:T(8,128)S(1)}, f32[128,256]{1,0:T(8,128)S(1)}, u32[]{:S(2)}, u32[]{:S(2)}) collective-permute-start(f32[128,256]{1,0:T(8,128)S(1)} %slice.9), channel_id=1, source_target_pairs={{0,8},{1,9},{2,10},{3,11},{4,12},{5,13},{6,14},{7,15},{8,0},{9,1},... | collective-permute-start | bytes 393224 | tf_op jit(solution)/shard_map/ppermute | solution.py:78
  20.9 4.9 %collective-permute-start.7 = (f32[128,256]{1,0:T(8,128)S(1)}, f32[128,256]{1,0:T(8,128)S(1)}, u32[]{:S(2)}, u32[]{:S(2)}) collective-permute-start(f32[128,256]{1,0:T(8,128)S(1)} %slice_add_fusion), channel_id=1, source_target_pairs={{0,3},{1,2},{2,11},{3,10},{4,7},{5,6},{6,15},{7,14},{8,1},{9,0},{1... | collective-permute-start | bytes 393224 | tf_op jit(solution)/shard_map/ppermute | solution.py:78
  22.3 5.0 %collective-permute-start.6 = (f32[128,256]{1,0:T(8,128)S(1)}, f32[128,256]{1,0:T(8,128)S(1)}, u32[]{:S(2)}, u32[]{:S(2)}) collective-permute-start(f32[128,256]{1,0:T(8,128)S(1)} %slice_add_fusion), channel_id=1, source_target_pairs={{0,2},{1,3},{2,10},{3,11},{4,6},{5,7},{6,14},{7,15},{8,0},{9,1},{1... | collective-permute-start | bytes 393224 | tf_op jit(solution)/shard_map/ppermute | solution.py:78

commit v2 on v1

--- a/solution.py
+++ b/solution.py
@@ -58,8 +58,8 @@
     return interface_panel - total
 
 
-def is_home(r, c):
-    return (r ^ c) & 1 == 0
+def home_parity(c):
+    return (c ^ (c >> 1)) & 1
 
 
 def route(target):
@@ -67,9 +67,8 @@
     for r in range(4):
         for c in range(4):
             for l in range(2):
-                to = target(r, c, l)
-                if to is not None:
-                    pairs.append((r * 8 + c * 2 + l, to[0] * 8 + to[1] * 2 + to[2]))
+                r_to, c_to, l_to = target(r, c, l)
+                pairs.append((r * 8 + c * 2 + l, r_to * 8 + c_to * 2 + l_to))
     return pairs
 
 
@@ -77,33 +76,33 @@
     def send(value, target):
         return lax.ppermute(value, MESH_AXES, route(target))
 
+    def fetch(value, source):
+        return lax.ppermute(value, MESH_AXES, [(a, b) for b, a in route(source)])
+
     b = coupling[0, 0]
     r = lax.axis_index("row")
     c = lax.axis_index("col")
-    home = is_home(r, c)
+    home = r % 2 == home_parity(c)
     aligned = r // 2 == c // 2
-    far = send(solved, lambda r, c, l: (r, c ^ 2, l) if is_home(r, c) else (r ^ 1, c ^ 3, l))
-    near = send(solved, lambda r, c, l: None if is_home(r, c) else (r ^ 1, c ^ 1, l))
+    near = fetch(solved, lambda r, c, l: (r & 2 | home_parity(c), c ^ (r ^ c) & 1, l))
+    far = fetch(solved, lambda r, c, l: (r & 2 | home_parity(c), c ^ 2 ^ (r ^ c) & 1, l))
     b_z = send(b, lambda r, c, l: (r, c ^ 1, l))
     b_x = send(b, lambda r, c, l: (r ^ 2, c, l))
     b_zx = send(b_z, lambda r, c, l: (r ^ 2, c, l))
-    far, near, b_z, b_x, b_zx = lax.optimization_barrier((far, near, b_z, b_x, b_zx))
-    here = jnp.where(home, solved, near)
+    near, far, b_z, b_x, b_zx = lax.optimization_barrier((near, far, b_z, b_x, b_zx))
+    y_own = jnp.where(aligned, near, far)
+    y_across = jnp.where(aligned, far, near)
+    theirs = multiply(jnp.where(home, b, b_z), y_own) + multiply(jnp.where(home, b_x, b_zx), y_across)
+    theirs = send(theirs, lambda r, c, l: (r ^ 1, c, l))
+    mine = multiply(jnp.where(home, b_z, b), y_own) + multiply(jnp.where(home, b_zx, b_x), y_across)
+    part = mine + theirs
 
-    def both(own, other):
-        return jnp.concatenate([jnp.where(home, other, own), jnp.where(home, own, other)], 1)
+    def to_owner(r, c, l):
+        return (r, c ^ 1, l) if r % 2 == home_parity(c) else (r ^ 1, c, l)
 
-    block_here = both(jnp.where(aligned, b, b_x), jnp.where(aligned, b_z, b_zx))
-    block_far = both(jnp.where(aligned, b_x, b), jnp.where(aligned, b_zx, b_z))
-    early = multiply(block_here, here)
-    early, far = lax.optimization_barrier((early, far))
-    total = early + multiply(block_far, far)
-    rows = b.shape[1]
-    part = total[:rows] + send(total[rows:], lambda r, c, l: (r ^ 1, c, l))
-    to_owner = lambda r, c, l: (r, c ^ 1, l) if is_home(r, c) else (r ^ 1, c, l)
-    one = send(part, to_owner)
-    two = send(part, lambda r, c, l: to_owner(r, c, l)[:2] + (1 - l,))
-    return interface_panel - one - two
+    other_layer = send(part, lambda r, c, l: to_owner(r, c, 1 - l))
+    this_layer = send(part, to_owner)
+    return interface_panel - other_layer - this_layer
 
 
 def solution(mesh):

time: 28 us -> 27.1 us (0.968)
  other arithmetic: 1.65 us -> 0.68 us
  waiting for transfers between devices: 15.3 us -> 14.8 us
  matrix products: 0.79 us -> 1.16 us
  starting transfers between devices: 10 us -> 10.3 us
    ppermute x0 -> x2, starting transfers between devices: none -> 5.06 us  [fetch(): return lax.ppermute(value, MESH_AXES, [(a, b) for b, a in route(source)])]
    ppermute x8 -> x6, starting transfers between devices: 10 us -> 5.25 us  [send(): return lax.ppermute(value, MESH_AXES, route(target))]
    ppermute x8 -> x6, waiting for transfers between devices: 15.3 us -> 12.5 us  [send(): return lax.ppermute(value, MESH_AXES, route(target))]
    ppermute x0 -> x2, waiting for transfers between devices: none -> 2.21 us  [fetch(): return lax.ppermute(value, MESH_AXES, [(a, b) for b, a in route(source)])]
    select_n x1 -> x0, other arithmetic: 0.95 us -> none  [both(): jnp.where(home, other, own)]
    dot_general x2 -> x4, matrix products: 0.79 us -> 1.16 us  [multiply(): lax.dot_general(block, solved, (((0,), (0,)), ((), ())), precision=lax.Pr...]
  transfers between devices with their start and end apart: 8 -> 8, of which waited for: 6 -> 6; matrix products, arithmetic and copies ran while one was open for 0% -> 1% of each run, Pallas kernels for 0% -> 0%
where the time goes in v2:
time: 27.1 us; the launch traced here: 27 us
  waiting for transfers between devices  14.8 us (55%)
  starting transfers between devices  10.3 us (38%)
  matrix products  1.16 us (4%)
  other arithmetic  0.68 us (3%)
    ppermute x6, waiting for transfers between devices, send(): return lax.ppermute(value, MESH_AXES, route(target))  12.5 us
    ppermute x6, starting transfers between devices, send(): return lax.ppermute(value, MESH_AXES, route(target))  5.25 us
    ppermute x2, starting transfers between devices, fetch(): return lax.ppermute(value, MESH_AXES, [(a, b) for b, a in route(source)])  5.06 us
    ppermute x2, waiting for transfers between devices, fetch(): return lax.ppermute(value, MESH_AXES, [(a, b) for b, a in route(source)])  2.21 us
    dot_general x4, matrix products, multiply(): lax.dot_general(block, solved, (((0,), (0,)), ((), ())), precision=lax.Pr...  1.16 us
    sub x1, other arithmetic, pairs_of_planes(): return interface_panel - other_layer - this_layer  0.68 us
  transfers between devices with their start and end apart: 8, of which 6 were waited for; matrix products, arithmetic and copies ran while one was open for 1% of the time, Pallas kernels for 0%

profile of v2, /device:TPU:1, one launch (start us, length us, event | category | flops | bytes accessed | tf_op | source)
XLA Modules:
  0.0 27.0 jit_solution(17062479323233368399)
XLA Ops:
  0.0 2.1 %collective-permute-start.2 = (f32[256,128]{1,0:T(8,128)}, f32[256,128]{1,0:T(8,128)S(1)}, u32[]{:S(2)}, u32[]{:S(2)}) collective-permute-start(f32[256,128]{1,0:T(8,128)} %bitcast.9), channel_id=1, source_target_pairs={{0,2},{1,3},{2,0},{3,1},{4,6},{5,7},{6,4},{7,5},{8,10},{9,11},{10,... | collective-permute-start | bytes 393224 | tf_op jit(solution)/shard_map/ppermute | solution.py:77
  2.1 3.1 %collective-permute-start.1 = (f32[256,256]{1,0:T(8,128)}, f32[256,256]{1,0:T(8,128)S(1)}, u32[]{:S(2)}, u32[]{:S(2)}) collective-permute-start(f32[256,256]{1,0:T(8,128)} %param.5), channel_id=1, source_target_pairs={{4,0},{5,1},{12,2},{13,3},{8,4},{9,5},{0,6},{1,7},{6,8},{7,9},{14,... | collective-permute-start | bytes 786440 | tf_op jit(solution)/shard_map/ppermute | solution.py:80
  5.3 1.9 %collective-permute-start = (f32[256,256]{1,0:T(8,128)}, f32[256,256]{1,0:T(8,128)S(1)}, u32[]{:S(2)}, u32[]{:S(2)}) collective-permute-start(f32[256,256]{1,0:T(8,128)} %param.5), channel_id=1, source_target_pairs={{0,0},{1,1},{8,2},{9,3},{12,4},{13,5},{4,6},{5,7},{2,8},{3,9},{10,... | collective-permute-start | bytes 786440 | tf_op jit(solution)/shard_map/ppermute | solution.py:80
  7.2 1.3 %collective-permute-start.3 = (f32[256,128]{1,0:T(8,128)}, f32[256,128]{1,0:T(8,128)S(1)}, u32[]{:S(2)}, u32[]{:S(2)}) collective-permute-start(f32[256,128]{1,0:T(8,128)} %bitcast.10), channel_id=1, source_target_pairs={{0,16},{1,17},{2,18},{3,19},{4,20},{5,21},{6,22},{7,23},{8,24},{9,... | collective-permute-start | bytes 393224 | tf_op jit(solution)/shard_map/ppermute | solution.py:77
  8.5 0.0 collective-permute-done.2
  8.5 0.3 collective-permute-start.4
  8.7 0.0 copy-start
  8.7 4.0 %collective-permute-done.3 = f32[256,128]{1,0:T(8,128)S(1)} collective-permute-done((f32[256,128]{1,0:T(8,128)}, f32[256,128]{1,0:T(8,128)S(1)}, u32[]{:S(2)}, u32[]{:S(2)}) %collective-permute-start.3) | collective-permute-done | bytes 131104 | tf_op jit(solution)/shard_map/ppermute | solution.py:77
  12.7 2.8 %collective-permute-done.4 = f32[256,128]{1,0:T(8,128)S(1)} collective-permute-done((f32[256,128]{1,0:T(8,128)S(1)}, f32[256,128]{1,0:T(8,128)S(1)}, u32[]{:S(2)}, u32[]{:S(2)}) %collective-permute-start.4) | collective-permute-done | bytes 131104 | tf_op jit(solution)/shard_map/ppermute | solution.py:77
  15.5 0.0 collective-permute-done.1
  15.5 2.2 %collective-permute-done = f32[256,256]{1,0:T(8,128)S(1)} collective-permute-done((f32[256,256]{1,0:T(8,128)}, f32[256,256]{1,0:T(8,128)S(1)}, u32[]{:S(2)}, u32[]{:S(2)}) %collective-permute-start) | collective-permute-done | bytes 262176 | tf_op jit(solution)/shard_map/ppermute | solution.py:80
  17.7 0.3 %fusion.1 = f32[128,256]{1,0:T(8,128)S(1)} fusion(f32[256,128]{1,0:T(8,128)S(1)} %collective-permute-done.3, f32[256,128]{1,0:T(8,128)S(1)} %collective-permute-done.4, f32[256,256]{1,0:T(8,128)S(1)} %collective-permute-done.1, f32[256,256]{1,0:T(8,128)S(1)} %collective-permute-done, pred[]{:T(512)S(6)} %eq.9, pred[]{:T(512)S(6)} %eq.8), kind=kOutput, calls=%fused_computation.4 | convolution fusion | flops 50429952 | bytes 917506 | tf_op jit(solution)/shard_map/dot_general | solution.py:10
  18.0 0.0 copy-done
  18.0 0.3 %convolution_add_fusion = f32[128,256]{1,0:T(8,128)S(1)} fusion(f32[128,256]{1,0:T(8,128)S(1)} %fusion.1, f32[256,128]{1,0:T(8,128)S(1)} %collective-permute-done.2, f32[256,256]{1,0:T(8,128)S(1)} %collective-permute-done, f32[256,256]{1,0:T(8,128)S(1)} %collective-permute-done.1, pred[]{:T(512)S(6)} %eq.9, pred[]{:T(512)S(6)} %eq.8, ...), kind=kOutput, calls=%fused_computation | convolution fusion | flops 50462720 | bytes 1048578 | tf_op jit(solution)/shard_map/dot_general | solution.py:10
  18.3 0.1 collective-permute-start.5
  18.4 0.3 %fusion.4 = f32[128,256]{1,0:T(8,128)S(1)} fusion(f32[256,128]{1,0:T(8,128)S(1)} %collective-permute-done.4, f32[256,128]{1,0:T(8,128)S(1)} %collective-permute-done.3, f32[256,256]{1,0:T(8,128)S(1)} %collective-permute-done.1, f32[256,256]{1,0:T(8,128)S(1)} %collective-permute-done, pred[]{:T(512)S(6)} %eq.9, pred[]{:T(512)S(6)} %eq.8), kind=kOutput, calls=%fused_computation.7 | convolution fusion | flops 50429952 | bytes 917506 | tf_op jit(solution)/shard_map/dot_general | solution.py:10
  18.7 0.0 copy-start.1
  18.7 1.0 %collective-permute-done.5 = f32[128,256]{1,0:T(8,128)S(1)} collective-permute-done((f32[128,256]{1,0:T(8,128)S(1)}, f32[128,256]{1,0:T(8,128)S(1)}, u32[]{:S(2)}, u32[]{:S(2)}) %collective-permute-start.5) | collective-permute-done | bytes 131104 | tf_op jit(solution)/shard_map/ppermute | solution.py:77
  19.8 0.3 %fusion = f32[128,256]{1,0:T(8,128)S(1)} fusion(f32[128,256]{1,0:T(8,128)S(1)} %collective-permute-done.5, f32[128,256]{1,0:T(8,128)S(1)} %fusion.4, f32[256,128]{1,0:T(8,128)S(1)} %collective-permute-done.2, f32[256,256]{1,0:T(8,128)S(1)} %collective-permute-done, f32[256,256]{1,0:T(8,128)S(1)} %collective-permute-done.1, pred[]{:T(512)S(6)} %eq.9, ...), kind=kOutput, calls=%fused_computation.2 | convolution fusion | flops 50495488 | bytes 1179650 | tf_op jit(solution)/shard_map/dot_general | solution.py:10
  20.1 0.2 collective-permute-start.7
  20.3 1.3 %collective-permute-start.6 = (f32[128,256]{1,0:T(8,128)S(1)}, f32[128,256]{1,0:T(8,128)S(1)}, u32[]{:S(2)}, u32[]{:S(2)}) collective-permute-start(f32[128,256]{1,0:T(8,128)S(1)} %fusion), channel_id=1, source_target_pairs={{0,3},{1,2},{2,11},{3,10},{4,13},{5,12},{6,5},{7,4},{8,1},{9,0},{1... | collective-permute-start | bytes 393224 | tf_op jit(solution)/shard_map/ppermute | solution.py:77
  21.6 2.6 %collective-permute-done.7 = f32[128,256]{1,0:T(8,128)S(1)} collective-permute-done((f32[128,256]{1,0:T(8,128)S(1)}, f32[128,256]{1,0:T(8,128)S(1)}, u32[]{:S(2)}, u32[]{:S(2)}) %collective-permute-start.7) | collective-permute-done | bytes 131104 | tf_op jit(solution)/shard_map/ppermute | solution.py:77
  24.2 2.1 %collective-permute-done.6 = f32[128,256]{1,0:T(8,128)S(1)} collective-permute-done((f32[128,256]{1,0:T(8,128)S(1)}, f32[128,256]{1,0:T(8,128)S(1)}, u32[]{:S(2)}, u32[]{:S(2)}) %collective-permute-start.6) | collective-permute-done | bytes 131104 | tf_op jit(solution)/shard_map/ppermute | solution.py:77
  26.3 0.0 copy-done.1
  26.3 0.7 %subtract_subtract_fusion = f32[128,256]{1,0:T(8,128)} fusion(f32[128,256]{1,0:T(8,128)S(1)} %collective-permute-done.7, f32[128,256]{1,0:T(8,128)S(1)} %copy-done.1, f32[128,256]{1,0:T(8,128)S(1)} %collective-permute-done.6), kind=kLoop, calls=%fused_computation.3 | loop fusion | flops 65536 | bytes 524288 | tf_op jit(solution)/shard_map/sub | solution.py:105
Async XLA Ops:
  0.0 8.5 %collective-permute-start.2 = (f32[256,128]{1,0:T(8,128)}, f32[256,128]{1,0:T(8,128)S(1)}, u32[]{:S(2)}, u32[]{:S(2)}) collective-permute-start(f32[256,128]{1,0:T(8,128)} %bitcast.9), channel_id=1, source_target_pairs={{0,2},{1,3},{2,0},{3,1},{4,6},{5,7},{6,4},{7,5},{8,10},{9,11},{10,... | collective-permute-start | bytes 393224 | tf_op jit(solution)/shard_map/ppermute | solution.py:77
  2.1 13.4 %collective-permute-start.1 = (f32[256,256]{1,0:T(8,128)}, f32[256,256]{1,0:T(8,128)S(1)}, u32[]{:S(2)}, u32[]{:S(2)}) collective-permute-start(f32[256,256]{1,0:T(8,128)} %param.5), channel_id=1, source_target_pairs={{4,0},{5,1},{12,2},{13,3},{8,4},{9,5},{0,6},{1,7},{6,8},{7,9},{14,... | collective-permute-start | bytes 786440 | tf_op jit(solution)/shard_map/ppermute | solution.py:80
  5.3 12.5 %collective-permute-start = (f32[256,256]{1,0:T(8,128)}, f32[256,256]{1,0:T(8,128)S(1)}, u32[]{:S(2)}, u32[]{:S(2)}) collective-permute-start(f32[256,256]{1,0:T(8,128)} %param.5), channel_id=1, source_target_pairs={{0,0},{1,1},{8,2},{9,3},{12,4},{13,5},{4,6},{5,7},{2,8},{3,9},{10,... | collective-permute-start | bytes 786440 | tf_op jit(solution)/shard_map/ppermute | solution.py:80
  7.2 5.5 %collective-permute-start.3 = (f32[256,128]{1,0:T(8,128)}, f32[256,128]{1,0:T(8,128)S(1)}, u32[]{:S(2)}, u32[]{:S(2)}) collective-permute-start(f32[256,128]{1,0:T(8,128)} %bitcast.10), channel_id=1, source_target_pairs={{0,16},{1,17},{2,18},{3,19},{4,20},{5,21},{6,22},{7,23},{8,24},{9,... | collective-permute-start | bytes 393224 | tf_op jit(solution)/shard_map/ppermute | solution.py:77
  8.5 7.1 %collective-permute-start.4 = (f32[256,128]{1,0:T(8,128)S(1)}, f32[256,128]{1,0:T(8,128)S(1)}, u32[]{:S(2)}, u32[]{:S(2)}) collective-permute-start(f32[256,128]{1,0:T(8,128)S(1)} %collective-permute-done.2), channel_id=1, source_target_pairs={{0,16},{1,17},{2,18},{3,19},{4,20},{5,21},{6,22},{7,23},{8,24},{9,... | collective-permute-start | bytes 393224 | tf_op jit(solution)/shard_map/ppermute | solution.py:77
  8.7 9.3 %copy-start = (f32[1,1,256,128]{3,2,1,0:T(8,128)S(1)}, f32[1,1,256,128]{3,2,1,0:T(8,128)}, u32[]{:S(2)}) copy-start(f32[1,1,256,128]{3,2,1,0:T(8,128)} %param.4) | copy-start | bytes 393220
  18.3 1.4 %collective-permute-start.5 = (f32[128,256]{1,0:T(8,128)S(1)}, f32[128,256]{1,0:T(8,128)S(1)}, u32[]{:S(2)}, u32[]{:S(2)}) collective-permute-start(f32[128,256]{1,0:T(8,128)S(1)} %convolution_add_fusion), channel_id=1, source_target_pairs={{0,8},{1,9},{2,10},{3,11},{4,12},{5,13},{6,14},{7,15},{8,0},{9,1},... | collective-permute-start | bytes 393224 | tf_op jit(solution)/shard_map/ppermute | solution.py:77
  18.7 7.6 %copy-start.1 = (f32[128,256]{1,0:T(8,128)S(1)}, f32[128,256]{1,0:T(8,128)}, u32[]{:S(2)}) copy-start(f32[128,256]{1,0:T(8,128)} %param.3) | copy-start | bytes 393220
  20.1 4.2 %collective-permute-start.7 = (f32[128,256]{1,0:T(8,128)S(1)}, f32[128,256]{1,0:T(8,128)S(1)}, u32[]{:S(2)}, u32[]{:S(2)}) collective-permute-start(f32[128,256]{1,0:T(8,128)S(1)} %fusion), channel_id=1, source_target_pairs={{0,2},{1,3},{2,10},{3,11},{4,12},{5,13},{6,4},{7,5},{8,0},{9,1},{1... | collective-permute-start | bytes 393224 | tf_op jit(solution)/shard_map/ppermute | solution.py:77
  20.3 6.0 %collective-permute-start.6 = (f32[128,256]{1,0:T(8,128)S(1)}, f32[128,256]{1,0:T(8,128)S(1)}, u32[]{:S(2)}, u32[]{:S(2)}) collective-permute-start(f32[128,256]{1,0:T(8,128)S(1)} %fusion), channel_id=1, source_target_pairs={{0,3},{1,2},{2,11},{3,10},{4,13},{5,12},{6,5},{7,4},{8,1},{9,0},{1... | collective-permute-start | bytes 393224 | tf_op jit(solution)/shard_map/ppermute | solution.py:77

commit v3 on v2

--- a/solution.py
+++ b/solution.py
@@ -58,8 +58,8 @@
     return interface_panel - total
 
 
-def home_parity(c):
-    return (c ^ (c >> 1)) & 1
+def is_home(r, c):
+    return (r ^ c) & 1 == 0
 
 
 def route(target):
@@ -76,16 +76,13 @@
     def send(value, target):
         return lax.ppermute(value, MESH_AXES, route(target))
 
-    def fetch(value, source):
-        return lax.ppermute(value, MESH_AXES, [(a, b) for b, a in route(source)])
-
     b = coupling[0, 0]
     r = lax.axis_index("row")
     c = lax.axis_index("col")
-    home = r % 2 == home_parity(c)
+    home = is_home(r, c)
     aligned = r // 2 == c // 2
-    near = fetch(solved, lambda r, c, l: (r & 2 | home_parity(c), c ^ (r ^ c) & 1, l))
-    far = fetch(solved, lambda r, c, l: (r & 2 | home_parity(c), c ^ 2 ^ (r ^ c) & 1, l))
+    near = send(solved, lambda r, c, l: (r, c, l) if is_home(r, c) else (r ^ 1, c ^ 1, l))
+    far = send(solved, lambda r, c, l: (r, c ^ 2, l) if is_home(r, c) else (r ^ 1, c ^ 3, l))
     b_z = send(b, lambda r, c, l: (r, c ^ 1, l))
     b_x = send(b, lambda r, c, l: (r ^ 2, c, l))
     b_zx = send(b_z, lambda r, c, l: (r ^ 2, c, l))
@@ -93,16 +90,17 @@
     y_own = jnp.where(aligned, near, far)
     y_across = jnp.where(aligned, far, near)
     theirs = multiply(jnp.where(home, b, b_z), y_own) + multiply(jnp.where(home, b_x, b_zx), y_across)
+    theirs, b_x, b_zx = lax.optimization_barrier((theirs, b_x, b_zx))
     theirs = send(theirs, lambda r, c, l: (r ^ 1, c, l))
     mine = multiply(jnp.where(home, b_z, b), y_own) + multiply(jnp.where(home, b_zx, b_x), y_across)
-    part = mine + theirs
+    part = lax.optimization_barrier(mine) + theirs
 
     def to_owner(r, c, l):
-        return (r, c ^ 1, l) if r % 2 == home_parity(c) else (r ^ 1, c, l)
+        return (r, c ^ 1, l) if is_home(r, c) else (r ^ 1, c, l)
 
+    this_layer = send(part, to_owner)
     other_layer = send(part, lambda r, c, l: to_owner(r, c, 1 - l))
-    this_layer = send(part, to_owner)
-    return interface_panel - other_layer - this_layer
+    return interface_panel - this_layer - other_layer
 
 
 def solution(mesh):

time: 27.1 us -> 26.8 us (0.989)
  starting transfers between devices: 10.3 us -> 10 us
    ppermute x2 -> x0, starting transfers between devices: 5.06 us -> none  [fetch(): return lax.ppermute(value, MESH_AXES, [(a, b) for b, a in route(source)])]
    ppermute x6 -> x8, starting transfers between devices: 5.25 us -> 10 us  [send(): return lax.ppermute(value, MESH_AXES, route(target))]
    ppermute x2 -> x0, waiting for transfers between devices: 2.21 us -> none  [fetch(): return lax.ppermute(value, MESH_AXES, [(a, b) for b, a in route(source)])]
    ppermute x6 -> x8, waiting for transfers between devices: 12.5 us -> 14.7 us  [send(): return lax.ppermute(value, MESH_AXES, route(target))]
  transfers between devices with their start and end apart: 8 -> 8, of which waited for: 6 -> 6; matrix products, arithmetic and copies ran while one was open for 1% -> 2% of each run, Pallas kernels for 0% -> 0%
where the time goes in v3:
time: 26.8 us; the launch traced here: 26.7 us
  waiting for transfers between devices  14.7 us (55%)
  starting transfers between devices  10 us (37%)
  matrix products  1.16 us (4%)
  other arithmetic  0.7 us (3%)
    ppermute x8, waiting for transfers between devices, send(): return lax.ppermute(value, MESH_AXES, route(target))  14.7 us
    ppermute x8, starting transfers between devices, send(): return lax.ppermute(value, MESH_AXES, route(target))  10 us
    dot_general x4, matrix products, multiply(): lax.dot_general(block, solved, (((0,), (0,)), ((), ())), precision=lax.Pr...  1.16 us
    sub x1, other arithmetic, pairs_of_planes(): return interface_panel - this_layer - other_layer  0.68 us
  transfers between devices with their start and end apart: 8, of which 6 were waited for; matrix products, arithmetic and copies ran while one was open for 2% of the time, Pallas kernels for 0%

profile of v3, /device:TPU:1, one launch (start us, length us, event | category | flops | bytes accessed | tf_op | source)
XLA Modules:
  0.0 26.7 jit_solution(653536706764414308)
XLA Ops:
  0.0 2.1 %collective-permute-start.2 = (f32[256,128]{1,0:T(8,128)}, f32[256,128]{1,0:T(8,128)S(1)}, u32[]{:S(2)}, u32[]{:S(2)}) collective-permute-start(f32[256,128]{1,0:T(8,128)} %bitcast.9), channel_id=1, source_target_pairs={{0,2},{1,3},{2,0},{3,1},{4,6},{5,7},{6,4},{7,5},{8,10},{9,11},{10,... | collective-permute-start | bytes 393224 | tf_op jit(solution)/shard_map/ppermute | solution.py:77
  2.1 3.0 %collective-permute-start.1 = (f32[256,256]{1,0:T(8,128)}, f32[256,256]{1,0:T(8,128)S(1)}, u32[]{:S(2)}, u32[]{:S(2)}) collective-permute-start(f32[256,256]{1,0:T(8,128)} %param.5), channel_id=1, source_target_pairs={{0,4},{1,5},{2,12},{3,13},{4,0},{5,1},{6,8},{7,9},{8,6},{9,7},{10,... | collective-permute-start | bytes 786440 | tf_op jit(solution)/shard_map/ppermute | solution.py:77
  5.2 1.9 %collective-permute-start = (f32[256,256]{1,0:T(8,128)}, f32[256,256]{1,0:T(8,128)S(1)}, u32[]{:S(2)}, u32[]{:S(2)}) collective-permute-start(f32[256,256]{1,0:T(8,128)} %param.5), channel_id=1, source_target_pairs={{0,0},{1,1},{2,8},{3,9},{4,4},{5,5},{6,12},{7,13},{8,2},{9,3},{10,... | collective-permute-start | bytes 786440 | tf_op jit(solution)/shard_map/ppermute | solution.py:77
  7.1 1.3 %collective-permute-start.3 = (f32[256,128]{1,0:T(8,128)}, f32[256,128]{1,0:T(8,128)S(1)}, u32[]{:S(2)}, u32[]{:S(2)}) collective-permute-start(f32[256,128]{1,0:T(8,128)} %bitcast.10), channel_id=1, source_target_pairs={{0,16},{1,17},{2,18},{3,19},{4,20},{5,21},{6,22},{7,23},{8,24},{9,... | collective-permute-start | bytes 393224 | tf_op jit(solution)/shard_map/ppermute | solution.py:77
  8.4 0.0 collective-permute-done.2
  8.4 0.3 collective-permute-start.4
  8.6 0.0 copy-start
  8.6 3.7 %collective-permute-done.3 = f32[256,128]{1,0:T(8,128)S(1)} collective-permute-done((f32[256,128]{1,0:T(8,128)}, f32[256,128]{1,0:T(8,128)S(1)}, u32[]{:S(2)}, u32[]{:S(2)}) %collective-permute-start.3) | collective-permute-done | bytes 131104 | tf_op jit(solution)/shard_map/ppermute | solution.py:77
  12.3 2.8 %collective-permute-done.4 = f32[256,128]{1,0:T(8,128)S(1)} collective-permute-done((f32[256,128]{1,0:T(8,128)S(1)}, f32[256,128]{1,0:T(8,128)S(1)}, u32[]{:S(2)}, u32[]{:S(2)}) %collective-permute-start.4) | collective-permute-done | bytes 131104 | tf_op jit(solution)/shard_map/ppermute | solution.py:77
  15.1 0.0 collective-permute-done.1
  15.1 2.6 %collective-permute-done = f32[256,256]{1,0:T(8,128)S(1)} collective-permute-done((f32[256,256]{1,0:T(8,128)}, f32[256,256]{1,0:T(8,128)S(1)}, u32[]{:S(2)}, u32[]{:S(2)}) %collective-permute-start) | collective-permute-done | bytes 262176 | tf_op jit(solution)/shard_map/ppermute | solution.py:77
  17.7 0.3 %fusion.2 = f32[128,256]{1,0:T(8,128)S(1)} fusion(f32[256,128]{1,0:T(8,128)S(1)} %collective-permute-done.3, f32[256,128]{1,0:T(8,128)S(1)} %collective-permute-done.4, f32[256,256]{1,0:T(8,128)S(1)} %collective-permute-done.1, f32[256,256]{1,0:T(8,128)S(1)} %collective-permute-done, pred[]{:T(512)S(6)} %eq.7, pred[]{:T(512)S(6)} %eq.6), kind=kOutput, calls=%fused_computation.5 | convolution fusion | flops 50429952 | bytes 917506 | tf_op jit(solution)/shard_map/dot_general | solution.py:10
  18.0 0.0 copy-done
  18.0 0.3 %convolution_add_fusion = f32[128,256]{1,0:T(8,128)S(1)} fusion(f32[128,256]{1,0:T(8,128)S(1)} %fusion.2, f32[256,128]{1,0:T(8,128)S(1)} %collective-permute-done.2, f32[256,256]{1,0:T(8,128)S(1)} %collective-permute-done, f32[256,256]{1,0:T(8,128)S(1)} %collective-permute-done.1, pred[]{:T(512)S(6)} %eq.7, pred[]{:T(512)S(6)} %eq.6, ...), kind=kOutput, calls=%fused_computation | convolution fusion | flops 50462720 | bytes 1048578 | tf_op jit(solution)/shard_map/dot_general | solution.py:10
  18.3 0.1 collective-permute-start.5
  18.4 0.3 %fusion = f32[128,256]{1,0:T(8,128)S(1)} fusion(f32[256,128]{1,0:T(8,128)S(1)} %collective-permute-done.4, f32[256,128]{1,0:T(8,128)S(1)} %collective-permute-done.3, f32[256,256]{1,0:T(8,128)S(1)} %collective-permute-done.1, f32[256,256]{1,0:T(8,128)S(1)} %collective-permute-done, pred[]{:T(512)S(6)} %eq.7, pred[]{:T(512)S(6)} %eq.6), kind=kOutput, calls=%fused_computation.3 | convolution fusion | flops 50429952 | bytes 917506 | tf_op jit(solution)/shard_map/dot_general | solution.py:10
  18.7 0.3 %convolution_add_fusion.1 = f32[128,256]{1,0:T(8,128)S(1)} fusion(f32[128,256]{1,0:T(8,128)S(1)} %fusion, f32[256,128]{1,0:T(8,128)S(1)} %collective-permute-done.2, f32[256,256]{1,0:T(8,128)S(1)} %collective-permute-done, f32[256,256]{1,0:T(8,128)S(1)} %collective-permute-done.1, pred[]{:T(512)S(6)} %eq.7, pred[]{:T(512)S(6)} %eq.6, ...), kind=kOutput, calls=%fused_computation.1 | convolution fusion | flops 50462720 | bytes 1048578 | tf_op jit(solution)/shard_map/dot_general | solution.py:10
  19.0 0.0 copy-start.1
  19.0 0.7 %collective-permute-done.5 = f32[128,256]{1,0:T(8,128)S(1)} collective-permute-done((f32[128,256]{1,0:T(8,128)S(1)}, f32[128,256]{1,0:T(8,128)S(1)}, u32[]{:S(2)}, u32[]{:S(2)}) %collective-permute-start.5) | collective-permute-done | bytes 131104 | tf_op jit(solution)/shard_map/ppermute | solution.py:77
  19.7 1.3 %collective-permute-start.7 = (f32[128,256]{1,0:T(8,128)S(1)}, f32[128,256]{1,0:T(8,128)S(1)}, u32[]{:S(2)}, u32[]{:S(2)}) collective-permute-start(f32[128,256]{1,0:T(8,128)S(1)} %add.13), channel_id=1, source_target_pairs={{0,3},{1,2},{2,11},{3,10},{4,7},{5,6},{6,15},{7,14},{8,1},{9,0},{1... | collective-permute-start | bytes 393224 | tf_op jit(solution)/shard_map/ppermute | solution.py:77
  21.1 0.0 collective-permute-start.6
  21.1 3.5 %collective-permute-done.7 = f32[128,256]{1,0:T(8,128)S(1)} collective-permute-done((f32[128,256]{1,0:T(8,128)S(1)}, f32[128,256]{1,0:T(8,128)S(1)}, u32[]{:S(2)}, u32[]{:S(2)}) %collective-permute-start.7) | collective-permute-done | bytes 131104 | tf_op jit(solution)/shard_map/ppermute | solution.py:77
  24.6 1.4 %collective-permute-done.6 = f32[128,256]{1,0:T(8,128)S(1)} collective-permute-done((f32[128,256]{1,0:T(8,128)S(1)}, f32[128,256]{1,0:T(8,128)S(1)}, u32[]{:S(2)}, u32[]{:S(2)}) %collective-permute-start.6) | collective-permute-done | bytes 131104 | tf_op jit(solution)/shard_map/ppermute | solution.py:77
  26.0 0.0 copy-done.1
  26.0 0.7 %subtract_subtract_fusion = f32[128,256]{1,0:T(8,128)} fusion(f32[128,256]{1,0:T(8,128)S(1)} %collective-permute-done.7, f32[128,256]{1,0:T(8,128)S(1)} %copy-done.1, f32[128,256]{1,0:T(8,128)S(1)} %collective-permute-done.6), kind=kLoop, calls=%fused_computation.2 | loop fusion | flops 65536 | bytes 524288 | tf_op jit(solution)/shard_map/sub | solution.py:103
  (1 shorter events, 0.0 us)
Async XLA Ops:
  0.0 8.4 %collective-permute-start.2 = (f32[256,128]{1,0:T(8,128)}, f32[256,128]{1,0:T(8,128)S(1)}, u32[]{:S(2)}, u32[]{:S(2)}) collective-permute-start(f32[256,128]{1,0:T(8,128)} %bitcast.9), channel_id=1, source_target_pairs={{0,2},{1,3},{2,0},{3,1},{4,6},{5,7},{6,4},{7,5},{8,10},{9,11},{10,... | collective-permute-start | bytes 393224 | tf_op jit(solution)/shard_map/ppermute | solution.py:77
  2.1 13.0 %collective-permute-start.1 = (f32[256,256]{1,0:T(8,128)}, f32[256,256]{1,0:T(8,128)S(1)}, u32[]{:S(2)}, u32[]{:S(2)}) collective-permute-start(f32[256,256]{1,0:T(8,128)} %param.5), channel_id=1, source_target_pairs={{0,4},{1,5},{2,12},{3,13},{4,0},{5,1},{6,8},{7,9},{8,6},{9,7},{10,... | collective-permute-start | bytes 786440 | tf_op jit(solution)/shard_map/ppermute | solution.py:77
  5.2 12.5 %collective-permute-start = (f32[256,256]{1,0:T(8,128)}, f32[256,256]{1,0:T(8,128)S(1)}, u32[]{:S(2)}, u32[]{:S(2)}) collective-permute-start(f32[256,256]{1,0:T(8,128)} %param.5), channel_id=1, source_target_pairs={{0,0},{1,1},{2,8},{3,9},{4,4},{5,5},{6,12},{7,13},{8,2},{9,3},{10,... | collective-permute-start | bytes 786440 | tf_op jit(solution)/shard_map/ppermute | solution.py:77
  7.1 5.2 %collective-permute-start.3 = (f32[256,128]{1,0:T(8,128)}, f32[256,128]{1,0:T(8,128)S(1)}, u32[]{:S(2)}, u32[]{:S(2)}) collective-permute-start(f32[256,128]{1,0:T(8,128)} %bitcast.10), channel_id=1, source_target_pairs={{0,16},{1,17},{2,18},{3,19},{4,20},{5,21},{6,22},{7,23},{8,24},{9,... | collective-permute-start | bytes 393224 | tf_op jit(solution)/shard_map/ppermute | solution.py:77
  8.4 6.8 %collective-permute-start.4 = (f32[256,128]{1,0:T(8,128)S(1)}, f32[256,128]{1,0:T(8,128)S(1)}, u32[]{:S(2)}, u32[]{:S(2)}) collective-permute-start(f32[256,128]{1,0:T(8,128)S(1)} %collective-permute-done.2), channel_id=1, source_target_pairs={{0,16},{1,17},{2,18},{3,19},{4,20},{5,21},{6,22},{7,23},{8,24},{9,... | collective-permute-start | bytes 393224 | tf_op jit(solution)/shard_map/ppermute | solution.py:77
  8.6 9.4 %copy-start = (f32[1,1,256,128]{3,2,1,0:T(8,128)S(1)}, f32[1,1,256,128]{3,2,1,0:T(8,128)}, u32[]{:S(2)}) copy-start(f32[1,1,256,128]{3,2,1,0:T(8,128)} %param.4) | copy-start | bytes 393220
  18.3 1.4 %collective-permute-start.5 = (f32[128,256]{1,0:T(8,128)S(1)}, f32[128,256]{1,0:T(8,128)S(1)}, u32[]{:S(2)}, u32[]{:S(2)}) collective-permute-start(f32[128,256]{1,0:T(8,128)S(1)} %convolution_add_fusion), channel_id=1, source_target_pairs={{0,8},{1,9},{2,10},{3,11},{4,12},{5,13},{6,14},{7,15},{8,0},{9,1},... | collective-permute-start | bytes 393224 | tf_op jit(solution)/shard_map/ppermute | solution.py:77
  19.0 7.0 %copy-start.1 = (f32[128,256]{1,0:T(8,128)S(1)}, f32[128,256]{1,0:T(8,128)}, u32[]{:S(2)}) copy-start(f32[128,256]{1,0:T(8,128)} %param.3) | copy-start | bytes 393220
  19.7 4.9 %collective-permute-start.7 = (f32[128,256]{1,0:T(8,128)S(1)}, f32[128,256]{1,0:T(8,128)S(1)}, u32[]{:S(2)}, u32[]{:S(2)}) collective-permute-start(f32[128,256]{1,0:T(8,128)S(1)} %add.13), channel_id=1, source_target_pairs={{0,3},{1,2},{2,11},{3,10},{4,7},{5,6},{6,15},{7,14},{8,1},{9,0},{1... | collective-permute-start | bytes 393224 | tf_op jit(solution)/shard_map/ppermute | solution.py:77
  21.1 5.0 %collective-permute-start.6 = (f32[128,256]{1,0:T(8,128)S(1)}, f32[128,256]{1,0:T(8,128)S(1)}, u32[]{:S(2)}, u32[]{:S(2)}) collective-permute-start(f32[128,256]{1,0:T(8,128)S(1)} %add.13), channel_id=1, source_target_pairs={{0,2},{1,3},{2,10},{3,11},{4,6},{5,7},{6,14},{7,15},{8,0},{9,1},{1... | collective-permute-start | bytes 393224 | tf_op jit(solution)/shard_map/ppermute | solution.py:77

commit v4 on v3

--- a/solution.py
+++ b/solution.py
@@ -81,26 +81,26 @@
     c = lax.axis_index("col")
     home = is_home(r, c)
     aligned = r // 2 == c // 2
-    near = send(solved, lambda r, c, l: (r, c, l) if is_home(r, c) else (r ^ 1, c ^ 1, l))
-    far = send(solved, lambda r, c, l: (r, c ^ 2, l) if is_home(r, c) else (r ^ 1, c ^ 3, l))
+    other = send(solved, lambda r, c, l: (r ^ 1, c, l))
+    near = send(other, lambda r, c, l: (r, c ^ 1, l) if is_home(r, c) else (r ^ 1, c, l))
+    far = send(other, lambda r, c, l: (r, c ^ 3, l) if is_home(r, c) else (r ^ 1, c ^ 2, l))
     b_z = send(b, lambda r, c, l: (r, c ^ 1, l))
     b_x = send(b, lambda r, c, l: (r ^ 2, c, l))
     b_zx = send(b_z, lambda r, c, l: (r ^ 2, c, l))
     near, far, b_z, b_x, b_zx = lax.optimization_barrier((near, far, b_z, b_x, b_zx))
     y_own = jnp.where(aligned, near, far)
     y_across = jnp.where(aligned, far, near)
-    theirs = multiply(jnp.where(home, b, b_z), y_own) + multiply(jnp.where(home, b_x, b_zx), y_across)
+    theirs = multiply(
+        jnp.concatenate([jnp.where(home, b, b_z), jnp.where(home, b_x, b_zx)]),
+        jnp.concatenate([y_own, y_across]),
+    )
     theirs, b_x, b_zx = lax.optimization_barrier((theirs, b_x, b_zx))
     theirs = send(theirs, lambda r, c, l: (r ^ 1, c, l))
     mine = multiply(jnp.where(home, b_z, b), y_own) + multiply(jnp.where(home, b_zx, b_x), y_across)
     part = lax.optimization_barrier(mine) + theirs
-
-    def to_owner(r, c, l):
-        return (r, c ^ 1, l) if is_home(r, c) else (r ^ 1, c, l)
-
-    this_layer = send(part, to_owner)
-    other_layer = send(part, lambda r, c, l: to_owner(r, c, 1 - l))
-    return interface_panel - this_layer - other_layer
+    one = send(part, lambda r, c, l: (r, c ^ 1, 1 - l) if is_home(r, c) else (r ^ 1, c, l))
+    two = send(part, lambda r, c, l: (r, c ^ 1, l) if is_home(r, c) else (r ^ 1, c, 1 - l))
+    return interface_panel - one - two
 
 
 def solution(mesh):

time: 26.8 us -> 26.4 us (0.985)
  waiting for transfers between devices: 14.7 us -> 11.4 us
  starting transfers between devices: 10 us -> 13 us
    ppermute x8 -> x9, waiting for transfers between devices: 14.7 us -> 11.4 us  [send(): return lax.ppermute(value, MESH_AXES, route(target))]
    ppermute x8 -> x9, starting transfers between devices: 10 us -> 13 us  [send(): return lax.ppermute(value, MESH_AXES, route(target))]
    dot_general x4 -> x3, matrix products: 1.16 us -> 0.99 us  [multiply(): lax.dot_general(block, solved, (((0,), (0,)), ((), ())), precision=lax.Pr...]
  transfers between devices with their start and end apart: 8 -> 9, of which waited for: 6 -> 5; matrix products, arithmetic and copies ran while one was open for 2% -> 2% of each run, Pallas kernels for 0% -> 0%
where the time goes in v4:
time: 26.4 us; the launch traced here: 26.2 us
  starting transfers between devices  13 us (49%)
  waiting for transfers between devices  11.4 us (43%)
  matrix products  0.99 us (4%)
  other arithmetic  0.77 us (3%)
    ppermute x9, starting transfers between devices, send(): return lax.ppermute(value, MESH_AXES, route(target))  13 us
    ppermute x9, waiting for transfers between devices, send(): return lax.ppermute(value, MESH_AXES, route(target))  11.4 us
    dot_general x3, matrix products, multiply(): lax.dot_general(block, solved, (((0,), (0,)), ((), ())), precision=lax.Pr...  0.99 us
    sub x1, other arithmetic, pairs_of_planes(): return interface_panel - one - two  0.68 us
  transfers between devices with their start and end apart: 9, of which 5 were waited for; matrix products, arithmetic and copies ran while one was open for 2% of the time, Pallas kernels for 0%

profile of v4, /device:TPU:1, one launch (start us, length us, event | category | flops | bytes accessed | tf_op | source)
XLA Modules:
  0.0 26.2 jit_solution(4578711777772252983)
XLA Ops:
  0.0 0.1 collective-permute-start
  0.1 2.7 %collective-permute-start.3 = (f32[256,128]{1,0:T(8,128)}, f32[256,128]{1,0:T(8,128)S(1)}, u32[]{:S(2)}, u32[]{:S(2)}) collective-permute-start(f32[256,128]{1,0:T(8,128)} %bitcast.8), channel_id=1, source_target_pairs={{0,2},{1,3},{2,0},{3,1},{4,6},{5,7},{6,4},{7,5},{8,10},{9,11},{10,... | collective-permute-start | bytes 393224 | tf_op jit(solution)/shard_map/ppermute | solution.py:77
  2.8 0.0 collective-permute-done
  2.8 2.6 %collective-permute-start.2 = (f32[256,256]{1,0:T(8,128)S(1)}, f32[256,256]{1,0:T(8,128)S(1)}, u32[]{:S(2)}, u32[]{:S(2)}) collective-permute-start(f32[256,256]{1,0:T(8,128)S(1)} %collective-permute-done), channel_id=1, source_target_pairs={{0,6},{1,7},{2,14},{3,15},{4,2},{5,3},{6,10},{7,11},{8,4},{9,5},{1... | collective-permute-start | bytes 786440 | tf_op jit(solution)/shard_map/ppermute | solution.py:77
  5.4 1.4 %collective-permute-start.1 = (f32[256,256]{1,0:T(8,128)S(1)}, f32[256,256]{1,0:T(8,128)S(1)}, u32[]{:S(2)}, u32[]{:S(2)}) collective-permute-start(f32[256,256]{1,0:T(8,128)S(1)} %collective-permute-done), channel_id=1, source_target_pairs={{0,2},{1,3},{2,10},{3,11},{4,6},{5,7},{6,14},{7,15},{8,0},{9,1},{1... | collective-permute-start | bytes 786440 | tf_op jit(solution)/shard_map/ppermute | solution.py:77
  6.9 1.2 %collective-permute-start.4 = (f32[256,128]{1,0:T(8,128)}, f32[256,128]{1,0:T(8,128)S(1)}, u32[]{:S(2)}, u32[]{:S(2)}) collective-permute-start(f32[256,128]{1,0:T(8,128)} %bitcast.9), channel_id=1, source_target_pairs={{0,16},{1,17},{2,18},{3,19},{4,20},{5,21},{6,22},{7,23},{8,24},{9,... | collective-permute-start | bytes 393224 | tf_op jit(solution)/shard_map/ppermute | solution.py:77
  8.1 0.0 collective-permute-done.3
  8.1 0.3 collective-permute-start.5
  8.3 0.0 copy-start
  8.3 3.5 %collective-permute-done.4 = f32[256,128]{1,0:T(8,128)S(1)} collective-permute-done((f32[256,128]{1,0:T(8,128)}, f32[256,128]{1,0:T(8,128)S(1)}, u32[]{:S(2)}, u32[]{:S(2)}) %collective-permute-start.4) | collective-permute-done | bytes 131104 | tf_op jit(solution)/shard_map/ppermute | solution.py:77
  11.8 2.8 %collective-permute-done.5 = f32[256,128]{1,0:T(8,128)S(1)} collective-permute-done((f32[256,128]{1,0:T(8,128)S(1)}, f32[256,128]{1,0:T(8,128)S(1)}, u32[]{:S(2)}, u32[]{:S(2)}) %collective-permute-start.5) | collective-permute-done | bytes 131104 | tf_op jit(solution)/shard_map/ppermute | solution.py:77
  14.7 0.0 collective-permute-done.2
  14.7 0.0 collective-permute-done.1
  14.7 0.0 copy-done
  14.8 0.4 %fusion = f32[128,256]{1,0:T(8,128)S(1)} fusion(f32[256,256]{1,0:T(8,128)S(1)} %get-tuple-element.22, f32[256,256]{1,0:T(8,128)S(1)} %get-tuple-element.21, f32[256,128]{1,0:T(8,128)S(1)} %get-tuple-element.23, f32[256,128]{1,0:T(8,128)S(1)} %get-tuple-element.24), kind=kOutput, calls=%fused_computation.1 | convolution fusion | flops 100859904 | bytes 917504 | tf_op jit(solution)/shard_map/dot_general | solution.py:10
  15.2 2.8 %collective-permute-start.6 = (f32[128,256]{1,0:T(8,128)S(1)}, f32[128,256]{1,0:T(8,128)S(1)}, u32[]{:S(2)}, u32[]{:S(2)}) collective-permute-start(f32[128,256]{1,0:T(8,128)S(1)} %fusion), channel_id=1, source_target_pairs={{0,8},{1,9},{2,10},{3,11},{4,12},{5,13},{6,14},{7,15},{8,0},{9,1},... | collective-permute-start | bytes 393224 | tf_op jit(solution)/shard_map/ppermute | solution.py:77
  17.9 0.3 %fusion.7 = f32[128,256]{1,0:T(8,128)S(1)} fusion(f32[256,256]{1,0:T(8,128)S(1)} %get-tuple-element.22, f32[256,128]{1,0:T(8,128)S(1)} %collective-permute-done.5, f32[256,128]{1,0:T(8,128)S(1)} %collective-permute-done.4, pred[]{:T(512)S(6)} %eq.6), kind=kOutput, calls=%fused_computation.9 | convolution fusion | flops 50364416 | bytes 655361 | tf_op jit(solution)/shard_map/dot_general | solution.py:10
  18.2 0.3 %convolution_add_fusion = f32[128,256]{1,0:T(8,128)S(1)} fusion(f32[128,256]{1,0:T(8,128)S(1)} %fusion.7, f32[256,256]{1,0:T(8,128)S(1)} %get-tuple-element.21, f32[256,128]{1,0:T(8,128)S(1)} %collective-permute-done.3, pred[]{:T(512)S(6)} %eq.6, f32[1,1,256,128]{3,2,1,0:T(8,128)S(1)} %copy-done), kind=kOutput, calls=%fused_computation | convolution fusion | flops 50397184 | bytes 786433 | tf_op jit(solution)/shard_map/dot_general | solution.py:10
  18.6 0.0 copy-start.1
  18.6 0.4 %collective-permute-done.6 = f32[128,256]{1,0:T(8,128)S(1)} collective-permute-done((f32[128,256]{1,0:T(8,128)S(1)}, f32[128,256]{1,0:T(8,128)S(1)}, u32[]{:S(2)}, u32[]{:S(2)}) %collective-permute-start.6) | collective-permute-done | bytes 131104 | tf_op jit(solution)/shard_map/ppermute | solution.py:77
  18.9 1.9 %collective-permute-start.8 = (f32[128,256]{1,0:T(8,128)S(1)}, f32[128,256]{1,0:T(8,128)S(1)}, u32[]{:S(2)}, u32[]{:S(2)}) collective-permute-start(f32[128,256]{1,0:T(8,128)S(1)} %add.9), channel_id=1, source_target_pairs={{0,2},{1,3},{2,11},{3,10},{4,6},{5,7},{6,15},{7,14},{8,1},{9,0},{1... | collective-permute-start | bytes 393224 | tf_op jit(solution)/shard_map/ppermute | solution.py:77
  20.8 0.0 collective-permute-start.7
  20.9 3.3 %collective-permute-done.8 = f32[128,256]{1,0:T(8,128)S(1)} collective-permute-done((f32[128,256]{1,0:T(8,128)S(1)}, f32[128,256]{1,0:T(8,128)S(1)}, u32[]{:S(2)}, u32[]{:S(2)}) %collective-permute-start.8) | collective-permute-done | bytes 131104 | tf_op jit(solution)/shard_map/ppermute | solution.py:77
  24.2 1.4 %collective-permute-done.7 = f32[128,256]{1,0:T(8,128)S(1)} collective-permute-done((f32[128,256]{1,0:T(8,128)S(1)}, f32[128,256]{1,0:T(8,128)S(1)}, u32[]{:S(2)}, u32[]{:S(2)}) %collective-permute-start.7) | collective-permute-done | bytes 131104 | tf_op jit(solution)/shard_map/ppermute | solution.py:77
  25.6 0.0 copy-done.1
  25.6 0.7 %subtract_subtract_fusion = f32[128,256]{1,0:T(8,128)} fusion(f32[128,256]{1,0:T(8,128)S(1)} %collective-permute-done.8, f32[128,256]{1,0:T(8,128)S(1)} %copy-done.1, f32[128,256]{1,0:T(8,128)S(1)} %collective-permute-done.7), kind=kLoop, calls=%fused_computation.8 | loop fusion | flops 65536 | bytes 524288 | tf_op jit(solution)/shard_map/sub | solution.py:103
  (3 shorter events, 0.1 us)
Async XLA Ops:
  0.0 2.8 %collective-permute-start = (f32[256,256]{1,0:T(8,128)}, f32[256,256]{1,0:T(8,128)S(1)}, u32[]{:S(2)}, u32[]{:S(2)}) collective-permute-start(f32[256,256]{1,0:T(8,128)} %param.5), channel_id=1, source_target_pairs={{0,8},{1,9},{2,10},{3,11},{4,12},{5,13},{6,14},{7,15},{8,0},{9,1},... | collective-permute-start | bytes 786440 | tf_op jit(solution)/shard_map/ppermute | solution.py:77
  0.1 8.0 %collective-permute-start.3 = (f32[256,128]{1,0:T(8,128)}, f32[256,128]{1,0:T(8,128)S(1)}, u32[]{:S(2)}, u32[]{:S(2)}) collective-permute-start(f32[256,128]{1,0:T(8,128)} %bitcast.8), channel_id=1, source_target_pairs={{0,2},{1,3},{2,0},{3,1},{4,6},{5,7},{6,4},{7,5},{8,10},{9,11},{10,... | collective-permute-start | bytes 393224 | tf_op jit(solution)/shard_map/ppermute | solution.py:77
  2.8 11.9 %collective-permute-start.2 = (f32[256,256]{1,0:T(8,128)S(1)}, f32[256,256]{1,0:T(8,128)S(1)}, u32[]{:S(2)}, u32[]{:S(2)}) collective-permute-start(f32[256,256]{1,0:T(8,128)S(1)} %collective-permute-done), channel_id=1, source_target_pairs={{0,6},{1,7},{2,14},{3,15},{4,2},{5,3},{6,10},{7,11},{8,4},{9,5},{1... | collective-permute-start | bytes 786440 | tf_op jit(solution)/shard_map/ppermute | solution.py:77
  5.4 9.2 %collective-permute-start.1 = (f32[256,256]{1,0:T(8,128)S(1)}, f32[256,256]{1,0:T(8,128)S(1)}, u32[]{:S(2)}, u32[]{:S(2)}) collective-permute-start(f32[256,256]{1,0:T(8,128)S(1)} %collective-permute-done), channel_id=1, source_target_pairs={{0,2},{1,3},{2,10},{3,11},{4,6},{5,7},{6,14},{7,15},{8,0},{9,1},{1... | collective-permute-start | bytes 786440 | tf_op jit(solution)/shard_map/ppermute | solution.py:77
  6.9 5.0 %collective-permute-start.4 = (f32[256,128]{1,0:T(8,128)}, f32[256,128]{1,0:T(8,128)S(1)}, u32[]{:S(2)}, u32[]{:S(2)}) collective-permute-start(f32[256,128]{1,0:T(8,128)} %bitcast.9), channel_id=1, source_target_pairs={{0,16},{1,17},{2,18},{3,19},{4,20},{5,21},{6,22},{7,23},{8,24},{9,... | collective-permute-start | bytes 393224 | tf_op jit(solution)/shard_map/ppermute | solution.py:77
  8.1 6.6 %collective-permute-start.5 = (f32[256,128]{1,0:T(8,128)S(1)}, f32[256,128]{1,0:T(8,128)S(1)}, u32[]{:S(2)}, u32[]{:S(2)}) collective-permute-start(f32[256,128]{1,0:T(8,128)S(1)} %collective-permute-done.3), channel_id=1, source_target_pairs={{0,16},{1,17},{2,18},{3,19},{4,20},{5,21},{6,22},{7,23},{8,24},{9,... | collective-permute-start | bytes 393224 | tf_op jit(solution)/shard_map/ppermute | solution.py:77
  8.3 6.4 %copy-start = (f32[1,1,256,128]{3,2,1,0:T(8,128)S(1)}, f32[1,1,256,128]{3,2,1,0:T(8,128)}, u32[]{:S(2)}) copy-start(f32[1,1,256,128]{3,2,1,0:T(8,128)} %param.4) | copy-start | bytes 393220
  15.2 3.8 %collective-permute-start.6 = (f32[128,256]{1,0:T(8,128)S(1)}, f32[128,256]{1,0:T(8,128)S(1)}, u32[]{:S(2)}, u32[]{:S(2)}) collective-permute-start(f32[128,256]{1,0:T(8,128)S(1)} %fusion), channel_id=1, source_target_pairs={{0,8},{1,9},{2,10},{3,11},{4,12},{5,13},{6,14},{7,15},{8,0},{9,1},... | collective-permute-start | bytes 393224 | tf_op jit(solution)/shard_map/ppermute | solution.py:77
  18.6 7.0 %copy-start.1 = (f32[128,256]{1,0:T(8,128)S(1)}, f32[128,256]{1,0:T(8,128)}, u32[]{:S(2)}) copy-start(f32[128,256]{1,0:T(8,128)} %param.3) | copy-start | bytes 393220
  18.9 5.2 %collective-permute-start.8 = (f32[128,256]{1,0:T(8,128)S(1)}, f32[128,256]{1,0:T(8,128)S(1)}, u32[]{:S(2)}, u32[]{:S(2)}) collective-permute-start(f32[128,256]{1,0:T(8,128)S(1)} %add.9), channel_id=1, source_target_pairs={{0,2},{1,3},{2,11},{3,10},{4,6},{5,7},{6,15},{7,14},{8,1},{9,0},{1... | collective-permute-start | bytes 393224 | tf_op jit(solution)/shard_map/ppermute | solution.py:77
  20.8 4.7 %collective-permute-start.7 = (f32[128,256]{1,0:T(8,128)S(1)}, f32[128,256]{1,0:T(8,128)S(1)}, u32[]{:S(2)}, u32[]{:S(2)}) collective-permute-start(f32[128,256]{1,0:T(8,128)S(1)} %add.9), channel_id=1, source_target_pairs={{0,3},{1,2},{2,10},{3,11},{4,7},{5,6},{6,14},{7,15},{8,0},{9,1},{1... | collective-permute-start | bytes 393224 | tf_op jit(solution)/shard_map/ppermute | solution.py:77

commit v5 on v4

--- a/solution.py
+++ b/solution.py
@@ -82,21 +82,17 @@
     home = is_home(r, c)
     aligned = r // 2 == c // 2
     other = send(solved, lambda r, c, l: (r ^ 1, c, l))
+    far = send(other, lambda r, c, l: (r, c ^ 3, l) if is_home(r, c) else (r ^ 1, c ^ 2, l))
     near = send(other, lambda r, c, l: (r, c ^ 1, l) if is_home(r, c) else (r ^ 1, c, l))
-    far = send(other, lambda r, c, l: (r, c ^ 3, l) if is_home(r, c) else (r ^ 1, c ^ 2, l))
     b_z = send(b, lambda r, c, l: (r, c ^ 1, l))
     b_x = send(b, lambda r, c, l: (r ^ 2, c, l))
     b_zx = send(b_z, lambda r, c, l: (r ^ 2, c, l))
     near, far, b_z, b_x, b_zx = lax.optimization_barrier((near, far, b_z, b_x, b_zx))
-    y_own = jnp.where(aligned, near, far)
-    y_across = jnp.where(aligned, far, near)
-    theirs = multiply(
-        jnp.concatenate([jnp.where(home, b, b_z), jnp.where(home, b_x, b_zx)]),
-        jnp.concatenate([y_own, y_across]),
-    )
+    y = jnp.concatenate([jnp.where(aligned, near, far), jnp.where(aligned, far, near)])
+    theirs = multiply(jnp.concatenate([jnp.where(home, b, b_z), jnp.where(home, b_x, b_zx)]), y)
     theirs, b_x, b_zx = lax.optimization_barrier((theirs, b_x, b_zx))
     theirs = send(theirs, lambda r, c, l: (r ^ 1, c, l))
-    mine = multiply(jnp.where(home, b_z, b), y_own) + multiply(jnp.where(home, b_zx, b_x), y_across)
+    mine = multiply(jnp.concatenate([jnp.where(home, b_z, b), jnp.where(home, b_zx, b_x)]), y)
     part = lax.optimization_barrier(mine) + theirs
     one = send(part, lambda r, c, l: (r, c ^ 1, 1 - l) if is_home(r, c) else (r ^ 1, c, l))
     two = send(part, lambda r, c, l: (r, c ^ 1, l) if is_home(r, c) else (r ^ 1, c, 1 - l))

time: 26.4 us -> 28.9 us (1.095); the launches traced: 26.2 us -> 28.4 us
  waiting for transfers between devices: 11.4 us -> 13.7 us
    ppermute x9, waiting for transfers between devices: 11.4 us -> 13.7 us  [send(): return lax.ppermute(value, MESH_AXES, route(target))]
    dot_general x3 -> x2, matrix products: 0.99 us -> 0.8 us  [multiply(): lax.dot_general(block, solved, (((0,), (0,)), ((), ())), precision=lax.Pr...]
  transfers between devices with their start and end apart: 9 -> 9, of which waited for: 5 -> 6; matrix products, arithmetic and copies ran while one was open for 2% -> 1% of each run, Pallas kernels for 0% -> 0%
where the time goes in v5:
time: 28.9 us; the launch traced here: 28.4 us
  waiting for transfers between devices  13.7 us (47%)
  starting transfers between devices  13.1 us (45%)
  matrix products  0.8 us (3%)
  other arithmetic  0.78 us (3%)
    ppermute x9, waiting for transfers between devices, send(): return lax.ppermute(value, MESH_AXES, route(target))  13.7 us
    ppermute x9, starting transfers between devices, send(): return lax.ppermute(value, MESH_AXES, route(target))  13.1 us
    dot_general x2, matrix products, multiply(): lax.dot_general(block, solved, (((0,), (0,)), ((), ())), precision=lax.Pr...  0.8 us
    sub x1, other arithmetic, pairs_of_planes(): return interface_panel - one - two  0.68 us
  transfers between devices with their start and end apart: 9, of which 6 were waited for; matrix products, arithmetic and copies ran while one was open for 1% of the time, Pallas kernels for 0%

profile of v5, /device:TPU:1, one launch (start us, length us, event | category | flops | bytes accessed | tf_op | source)
XLA Modules:
  0.0 28.4 jit_solution(236913062169831562)
XLA Ops:
  0.0 0.1 collective-permute-start
  0.1 2.7 %collective-permute-start.3 = (f32[256,128]{1,0:T(8,128)}, f32[256,128]{1,0:T(8,128)S(1)}, u32[]{:S(2)}, u32[]{:S(2)}) collective-permute-start(f32[256,128]{1,0:T(8,128)} %bitcast.3), channel_id=1, source_target_pairs={{0,2},{1,3},{2,0},{3,1},{4,6},{5,7},{6,4},{7,5},{8,10},{9,11},{10,... | collective-permute-start | bytes 393224 | tf_op jit(solution)/shard_map/ppermute | solution.py:77
  2.8 0.0 collective-permute-done
  2.8 0.3 collective-permute-start.1
  3.1 3.9 %collective-permute-start.2 = (f32[256,256]{1,0:T(8,128)S(1)}, f32[256,256]{1,0:T(8,128)S(1)}, u32[]{:S(2)}, u32[]{:S(2)}) collective-permute-start(f32[256,256]{1,0:T(8,128)S(1)} %collective-permute-done), channel_id=1, source_target_pairs={{0,6},{1,7},{2,14},{3,15},{4,2},{5,3},{6,10},{7,11},{8,4},{9,5},{1... | collective-permute-start | bytes 786440 | tf_op jit(solution)/shard_map/ppermute | solution.py:77
  7.0 1.2 %collective-permute-start.4 = (f32[256,128]{1,0:T(8,128)}, f32[256,128]{1,0:T(8,128)S(1)}, u32[]{:S(2)}, u32[]{:S(2)}) collective-permute-start(f32[256,128]{1,0:T(8,128)} %bitcast.4), channel_id=1, source_target_pairs={{0,16},{1,17},{2,18},{3,19},{4,20},{5,21},{6,22},{7,23},{8,24},{9,... | collective-permute-start | bytes 393224 | tf_op jit(solution)/shard_map/ppermute | solution.py:77
  8.2 0.0 collective-permute-done.3
  8.2 0.3 collective-permute-start.5
  8.5 0.0 copy-start
  8.5 3.9 %collective-permute-done.4 = f32[256,128]{1,0:T(8,128)S(1)} collective-permute-done((f32[256,128]{1,0:T(8,128)}, f32[256,128]{1,0:T(8,128)S(1)}, u32[]{:S(2)}, u32[]{:S(2)}) %collective-permute-start.4) | collective-permute-done | bytes 131104 | tf_op jit(solution)/shard_map/ppermute | solution.py:77
  12.4 2.8 %collective-permute-done.5 = f32[256,128]{1,0:T(8,128)S(1)} collective-permute-done((f32[256,128]{1,0:T(8,128)S(1)}, f32[256,128]{1,0:T(8,128)S(1)}, u32[]{:S(2)}, u32[]{:S(2)}) %collective-permute-start.5) | collective-permute-done | bytes 131104 | tf_op jit(solution)/shard_map/ppermute | solution.py:77
  15.2 0.0 collective-permute-done.1
  15.2 2.3 %collective-permute-done.2 = f32[256,256]{1,0:T(8,128)S(1)} collective-permute-done((f32[256,256]{1,0:T(8,128)S(1)}, f32[256,256]{1,0:T(8,128)S(1)}, u32[]{:S(2)}, u32[]{:S(2)}) %collective-permute-start.2) | collective-permute-done | bytes 262176 | tf_op jit(solution)/shard_map/ppermute | solution.py:77
  17.5 0.0 copy-done
  17.6 0.4 %fusion.1 = f32[128,256]{1,0:T(8,128)S(1)} fusion(f32[256,256]{1,0:T(8,128)S(1)} %get-tuple-element.22, f32[256,256]{1,0:T(8,128)S(1)} %get-tuple-element.21, f32[256,128]{1,0:T(8,128)S(1)} %get-tuple-element.25, f32[256,128]{1,0:T(8,128)S(1)} %get-tuple-element.24), kind=kOutput, calls=%fused_computation.2 | convolution fusion | flops 100859904 | bytes 917504 | tf_op jit(solution)/shard_map/dot_general | solution.py:10
  18.0 2.3 %collective-permute-start.6 = (f32[128,256]{1,0:T(8,128)S(1)}, f32[128,256]{1,0:T(8,128)S(1)}, u32[]{:S(2)}, u32[]{:S(2)}) collective-permute-start(f32[128,256]{1,0:T(8,128)S(1)} %fusion.1), channel_id=1, source_target_pairs={{0,8},{1,9},{2,10},{3,11},{4,12},{5,13},{6,14},{7,15},{8,0},{9,1},... | collective-permute-start | bytes 393224 | tf_op jit(solution)/shard_map/ppermute | solution.py:77
  20.3 0.4 %fusion = f32[128,256]{1,0:T(8,128)S(1)} fusion(f32[256,256]{1,0:T(8,128)S(1)} %get-tuple-element.22, f32[256,256]{1,0:T(8,128)S(1)} %get-tuple-element.21, f32[256,128]{1,0:T(8,128)S(1)} %broadcast_select_fusion.2, f32[256,128]{1,0:T(8,128)S(1)} %get-tuple-element.23), kind=kOutput, calls=%fused_computation.1 | convolution fusion | flops 100859904 | bytes 917504 | tf_op jit(solution)/shard_map/dot_general | solution.py:10
  20.7 0.0 copy-start.1
  20.7 0.6 %collective-permute-done.6 = f32[128,256]{1,0:T(8,128)S(1)} collective-permute-done((f32[128,256]{1,0:T(8,128)S(1)}, f32[128,256]{1,0:T(8,128)S(1)}, u32[]{:S(2)}, u32[]{:S(2)}) %collective-permute-start.6) | collective-permute-done | bytes 131104 | tf_op jit(solution)/shard_map/ppermute | solution.py:77
  21.3 0.4 %collective-permute-start.7 = (f32[128,256]{1,0:T(8,128)S(1)}, f32[128,256]{1,0:T(8,128)S(1)}, u32[]{:S(2)}, u32[]{:S(2)}) collective-permute-start(f32[128,256]{1,0:T(8,128)S(1)} %add.5), channel_id=1, source_target_pairs={{0,3},{1,2},{2,10},{3,11},{4,7},{5,6},{6,14},{7,15},{8,0},{9,1},{1... | collective-permute-start | bytes 393224 | tf_op jit(solution)/shard_map/ppermute | solution.py:77
  21.7 1.9 %collective-permute-start.8 = (f32[128,256]{1,0:T(8,128)S(1)}, f32[128,256]{1,0:T(8,128)S(1)}, u32[]{:S(2)}, u32[]{:S(2)}) collective-permute-start(f32[128,256]{1,0:T(8,128)S(1)} %add.5), channel_id=1, source_target_pairs={{0,2},{1,3},{2,11},{3,10},{4,6},{5,7},{6,15},{7,14},{8,1},{9,0},{1... | collective-permute-start | bytes 393224 | tf_op jit(solution)/shard_map/ppermute | solution.py:77
  23.6 2.5 %collective-permute-done.7 = f32[128,256]{1,0:T(8,128)S(1)} collective-permute-done((f32[128,256]{1,0:T(8,128)S(1)}, f32[128,256]{1,0:T(8,128)S(1)}, u32[]{:S(2)}, u32[]{:S(2)}) %collective-permute-start.7) | collective-permute-done | bytes 131104 | tf_op jit(solution)/shard_map/ppermute | solution.py:77
  26.1 1.7 %collective-permute-done.8 = f32[128,256]{1,0:T(8,128)S(1)} collective-permute-done((f32[128,256]{1,0:T(8,128)S(1)}, f32[128,256]{1,0:T(8,128)S(1)}, u32[]{:S(2)}, u32[]{:S(2)}) %collective-permute-start.8) | collective-permute-done | bytes 131104 | tf_op jit(solution)/shard_map/ppermute | solution.py:77
  27.8 0.0 copy-done.1
  27.8 0.7 %subtract_subtract_fusion = f32[128,256]{1,0:T(8,128)} fusion(f32[128,256]{1,0:T(8,128)S(1)} %collective-permute-done.8, f32[128,256]{1,0:T(8,128)S(1)} %copy-done.1, f32[128,256]{1,0:T(8,128)S(1)} %collective-permute-done.7), kind=kLoop, calls=%fused_computation.9 | loop fusion | flops 65536 | bytes 524288 | tf_op jit(solution)/shard_map/sub | solution.py:99
  (4 shorter events, 0.1 us)
Async XLA Ops:
  0.0 2.8 %collective-permute-start = (f32[256,256]{1,0:T(8,128)}, f32[256,256]{1,0:T(8,128)S(1)}, u32[]{:S(2)}, u32[]{:S(2)}) collective-permute-start(f32[256,256]{1,0:T(8,128)} %param.5), channel_id=1, source_target_pairs={{0,8},{1,9},{2,10},{3,11},{4,12},{5,13},{6,14},{7,15},{8,0},{9,1},... | collective-permute-start | bytes 786440 | tf_op jit(solution)/shard_map/ppermute | solution.py:77
  0.1 8.2 %collective-permute-start.3 = (f32[256,128]{1,0:T(8,128)}, f32[256,128]{1,0:T(8,128)S(1)}, u32[]{:S(2)}, u32[]{:S(2)}) collective-permute-start(f32[256,128]{1,0:T(8,128)} %bitcast.3), channel_id=1, source_target_pairs={{0,2},{1,3},{2,0},{3,1},{4,6},{5,7},{6,4},{7,5},{8,10},{9,11},{10,... | collective-permute-start | bytes 393224 | tf_op jit(solution)/shard_map/ppermute | solution.py:77
  2.8 12.4 %collective-permute-start.1 = (f32[256,256]{1,0:T(8,128)S(1)}, f32[256,256]{1,0:T(8,128)S(1)}, u32[]{:S(2)}, u32[]{:S(2)}) collective-permute-start(f32[256,256]{1,0:T(8,128)S(1)} %collective-permute-done), channel_id=1, source_target_pairs={{0,2},{1,3},{2,10},{3,11},{4,6},{5,7},{6,14},{7,15},{8,0},{9,1},{1... | collective-permute-start | bytes 786440 | tf_op jit(solution)/shard_map/ppermute | solution.py:77
  3.1 14.4 %collective-permute-start.2 = (f32[256,256]{1,0:T(8,128)S(1)}, f32[256,256]{1,0:T(8,128)S(1)}, u32[]{:S(2)}, u32[]{:S(2)}) collective-permute-start(f32[256,256]{1,0:T(8,128)S(1)} %collective-permute-done), channel_id=1, source_target_pairs={{0,6},{1,7},{2,14},{3,15},{4,2},{5,3},{6,10},{7,11},{8,4},{9,5},{1... | collective-permute-start | bytes 786440 | tf_op jit(solution)/shard_map/ppermute | solution.py:77
  7.0 5.4 %collective-permute-start.4 = (f32[256,128]{1,0:T(8,128)}, f32[256,128]{1,0:T(8,128)S(1)}, u32[]{:S(2)}, u32[]{:S(2)}) collective-permute-start(f32[256,128]{1,0:T(8,128)} %bitcast.4), channel_id=1, source_target_pairs={{0,16},{1,17},{2,18},{3,19},{4,20},{5,21},{6,22},{7,23},{8,24},{9,... | collective-permute-start | bytes 393224 | tf_op jit(solution)/shard_map/ppermute | solution.py:77
  8.2 7.0 %collective-permute-start.5 = (f32[256,128]{1,0:T(8,128)S(1)}, f32[256,128]{1,0:T(8,128)S(1)}, u32[]{:S(2)}, u32[]{:S(2)}) collective-permute-start(f32[256,128]{1,0:T(8,128)S(1)} %collective-permute-done.3), channel_id=1, source_target_pairs={{0,16},{1,17},{2,18},{3,19},{4,20},{5,21},{6,22},{7,23},{8,24},{9,... | collective-permute-start | bytes 393224 | tf_op jit(solution)/shard_map/ppermute | solution.py:77
  8.5 9.0 %copy-start = (f32[1,1,256,128]{3,2,1,0:T(8,128)S(1)}, f32[1,1,256,128]{3,2,1,0:T(8,128)}, u32[]{:S(2)}) copy-start(f32[1,1,256,128]{3,2,1,0:T(8,128)} %param.4) | copy-start | bytes 393220
  18.0 3.3 %collective-permute-start.6 = (f32[128,256]{1,0:T(8,128)S(1)}, f32[128,256]{1,0:T(8,128)S(1)}, u32[]{:S(2)}, u32[]{:S(2)}) collective-permute-start(f32[128,256]{1,0:T(8,128)S(1)} %fusion.1), channel_id=1, source_target_pairs={{0,8},{1,9},{2,10},{3,11},{4,12},{5,13},{6,14},{7,15},{8,0},{9,1},... | collective-permute-start | bytes 393224 | tf_op jit(solution)/shard_map/ppermute | solution.py:77
  20.7 7.1 %copy-start.1 = (f32[128,256]{1,0:T(8,128)S(1)}, f32[128,256]{1,0:T(8,128)}, u32[]{:S(2)}) copy-start(f32[128,256]{1,0:T(8,128)} %param.3) | copy-start | bytes 393220
  21.3 4.8 %collective-permute-start.7 = (f32[128,256]{1,0:T(8,128)S(1)}, f32[128,256]{1,0:T(8,128)S(1)}, u32[]{:S(2)}, u32[]{:S(2)}) collective-permute-start(f32[128,256]{1,0:T(8,128)S(1)} %add.5), channel_id=1, source_target_pairs={{0,3},{1,2},{2,10},{3,11},{4,7},{5,6},{6,14},{7,15},{8,0},{9,1},{1... | collective-permute-start | bytes 393224 | tf_op jit(solution)/shard_map/ppermute | solution.py:77
  21.7 6.1 %collective-permute-start.8 = (f32[128,256]{1,0:T(8,128)S(1)}, f32[128,256]{1,0:T(8,128)S(1)}, u32[]{:S(2)}, u32[]{:S(2)}) collective-permute-start(f32[128,256]{1,0:T(8,128)S(1)} %add.5), channel_id=1, source_target_pairs={{0,2},{1,3},{2,11},{3,10},{4,6},{5,7},{6,15},{7,14},{8,1},{9,0},{1... | collective-permute-start | bytes 393224 | tf_op jit(solution)/shard_map/ppermute | solution.py:77

commit v6 on v5

--- a/solution.py
+++ b/solution.py
@@ -87,7 +87,7 @@
     b_z = send(b, lambda r, c, l: (r, c ^ 1, l))
     b_x = send(b, lambda r, c, l: (r ^ 2, c, l))
     b_zx = send(b_z, lambda r, c, l: (r ^ 2, c, l))
-    near, far, b_z, b_x, b_zx = lax.optimization_barrier((near, far, b_z, b_x, b_zx))
+    far, near, b_z, b_x, b_zx = lax.optimization_barrier((far, near, b_z, b_x, b_zx))
     y = jnp.concatenate([jnp.where(aligned, near, far), jnp.where(aligned, far, near)])
     theirs = multiply(jnp.concatenate([jnp.where(home, b, b_z), jnp.where(home, b_x, b_zx)]), y)
     theirs, b_x, b_zx = lax.optimization_barrier((theirs, b_x, b_zx))

time: 28.9 us -> 27.1 us (0.938)
  waiting for transfers between devices: 13.7 us -> 10.9 us
  starting transfers between devices: 13.1 us -> 14 us
    ppermute x9, waiting for transfers between devices: 13.7 us -> 10.9 us  [send(): return lax.ppermute(value, MESH_AXES, route(target))]
    ppermute x9, starting transfers between devices: 13.1 us -> 14 us  [send(): return lax.ppermute(value, MESH_AXES, route(target))]
  transfers between devices with their start and end apart: 9 -> 9, of which waited for: 6 -> 5; matrix products, arithmetic and copies ran while one was open for 1% -> 2% of each run, Pallas kernels for 0% -> 0%
where the time goes in v6:
time: 27.1 us; the launch traced here: 26.5 us
  starting transfers between devices  14 us (52%)
  waiting for transfers between devices  10.9 us (40%)
  matrix products  0.8 us (3%)
  other arithmetic  0.78 us (3%)
    ppermute x9, starting transfers between devices, send(): return lax.ppermute(value, MESH_AXES, route(target))  14 us
    ppermute x9, waiting for transfers between devices, send(): return lax.ppermute(value, MESH_AXES, route(target))  10.9 us
    dot_general x2, matrix products, multiply(): lax.dot_general(block, solved, (((0,), (0,)), ((), ())), precision=lax.Pr...  0.8 us
    sub x1, other arithmetic, pairs_of_planes(): return interface_panel - one - two  0.68 us
  transfers between devices with their start and end apart: 9, of which 5 were waited for; matrix products, arithmetic and copies ran while one was open for 2% of the time, Pallas kernels for 0%

profile of v6, /device:TPU:1, one launch (start us, length us, event | category | flops | bytes accessed | tf_op | source)
XLA Modules:
  0.0 26.5 jit_solution(16961537063872741884)
XLA Ops:
  0.0 0.1 collective-permute-start
  0.1 2.7 %collective-permute-start.3 = (f32[256,128]{1,0:T(8,128)}, f32[256,128]{1,0:T(8,128)S(1)}, u32[]{:S(2)}, u32[]{:S(2)}) collective-permute-start(f32[256,128]{1,0:T(8,128)} %bitcast.3), channel_id=1, source_target_pairs={{0,2},{1,3},{2,0},{3,1},{4,6},{5,7},{6,4},{7,5},{8,10},{9,11},{10,... | collective-permute-start | bytes 393224 | tf_op jit(solution)/shard_map/ppermute | solution.py:77
  2.8 0.0 collective-permute-done
  2.8 2.6 %collective-permute-start.1 = (f32[256,256]{1,0:T(8,128)S(1)}, f32[256,256]{1,0:T(8,128)S(1)}, u32[]{:S(2)}, u32[]{:S(2)}) collective-permute-start(f32[256,256]{1,0:T(8,128)S(1)} %collective-permute-done), channel_id=1, source_target_pairs={{0,6},{1,7},{2,14},{3,15},{4,2},{5,3},{6,10},{7,11},{8,4},{9,5},{1... | collective-permute-start | bytes 786440 | tf_op jit(solution)/shard_map/ppermute | solution.py:77
  5.4 1.4 %collective-permute-start.2 = (f32[256,256]{1,0:T(8,128)S(1)}, f32[256,256]{1,0:T(8,128)S(1)}, u32[]{:S(2)}, u32[]{:S(2)}) collective-permute-start(f32[256,256]{1,0:T(8,128)S(1)} %collective-permute-done), channel_id=1, source_target_pairs={{0,2},{1,3},{2,10},{3,11},{4,6},{5,7},{6,14},{7,15},{8,0},{9,1},{1... | collective-permute-start | bytes 786440 | tf_op jit(solution)/shard_map/ppermute | solution.py:77
  6.9 1.2 %collective-permute-start.4 = (f32[256,128]{1,0:T(8,128)}, f32[256,128]{1,0:T(8,128)S(1)}, u32[]{:S(2)}, u32[]{:S(2)}) collective-permute-start(f32[256,128]{1,0:T(8,128)} %bitcast.4), channel_id=1, source_target_pairs={{0,16},{1,17},{2,18},{3,19},{4,20},{5,21},{6,22},{7,23},{8,24},{9,... | collective-permute-start | bytes 393224 | tf_op jit(solution)/shard_map/ppermute | solution.py:77
  8.1 0.0 collective-permute-done.3
  8.1 0.3 collective-permute-start.5
  8.3 0.0 copy-start
  8.3 3.5 %collective-permute-done.4 = f32[256,128]{1,0:T(8,128)S(1)} collective-permute-done((f32[256,128]{1,0:T(8,128)}, f32[256,128]{1,0:T(8,128)S(1)}, u32[]{:S(2)}, u32[]{:S(2)}) %collective-permute-start.4) | collective-permute-done | bytes 131104 | tf_op jit(solution)/shard_map/ppermute | solution.py:77
  11.8 2.8 %collective-permute-done.5 = f32[256,128]{1,0:T(8,128)S(1)} collective-permute-done((f32[256,128]{1,0:T(8,128)S(1)}, f32[256,128]{1,0:T(8,128)S(1)}, u32[]{:S(2)}, u32[]{:S(2)}) %collective-permute-start.5) | collective-permute-done | bytes 131104 | tf_op jit(solution)/shard_map/ppermute | solution.py:77
  14.7 0.0 collective-permute-done.1
  14.7 0.0 collective-permute-done.2
  14.7 0.0 copy-done
  14.8 0.4 %fusion.1 = f32[128,256]{1,0:T(8,128)S(1)} fusion(f32[256,256]{1,0:T(8,128)S(1)} %get-tuple-element.22, f32[256,256]{1,0:T(8,128)S(1)} %get-tuple-element.21, f32[256,128]{1,0:T(8,128)S(1)} %get-tuple-element.25, f32[256,128]{1,0:T(8,128)S(1)} %get-tuple-element.24), kind=kOutput, calls=%fused_computation.2 | convolution fusion | flops 100859904 | bytes 917504 | tf_op jit(solution)/shard_map/dot_general | solution.py:10
  15.2 2.8 %collective-permute-start.6 = (f32[128,256]{1,0:T(8,128)S(1)}, f32[128,256]{1,0:T(8,128)S(1)}, u32[]{:S(2)}, u32[]{:S(2)}) collective-permute-start(f32[128,256]{1,0:T(8,128)S(1)} %fusion.1), channel_id=1, source_target_pairs={{0,8},{1,9},{2,10},{3,11},{4,12},{5,13},{6,14},{7,15},{8,0},{9,1},... | collective-permute-start | bytes 393224 | tf_op jit(solution)/shard_map/ppermute | solution.py:77
  18.0 0.4 %fusion = f32[128,256]{1,0:T(8,128)S(1)} fusion(f32[256,256]{1,0:T(8,128)S(1)} %get-tuple-element.22, f32[256,256]{1,0:T(8,128)S(1)} %get-tuple-element.21, f32[256,128]{1,0:T(8,128)S(1)} %broadcast_select_fusion.2, f32[256,128]{1,0:T(8,128)S(1)} %get-tuple-element.23), kind=kOutput, calls=%fused_computation.1 | convolution fusion | flops 100859904 | bytes 917504 | tf_op jit(solution)/shard_map/dot_general | solution.py:10
  18.4 0.0 copy-start.1
  18.4 0.6 %collective-permute-done.6 = f32[128,256]{1,0:T(8,128)S(1)} collective-permute-done((f32[128,256]{1,0:T(8,128)S(1)}, f32[128,256]{1,0:T(8,128)S(1)}, u32[]{:S(2)}, u32[]{:S(2)}) %collective-permute-start.6) | collective-permute-done | bytes 131104 | tf_op jit(solution)/shard_map/ppermute | solution.py:77
  19.0 0.4 %collective-permute-start.7 = (f32[128,256]{1,0:T(8,128)S(1)}, f32[128,256]{1,0:T(8,128)S(1)}, u32[]{:S(2)}, u32[]{:S(2)}) collective-permute-start(f32[128,256]{1,0:T(8,128)S(1)} %add.5), channel_id=1, source_target_pairs={{0,3},{1,2},{2,10},{3,11},{4,7},{5,6},{6,14},{7,15},{8,0},{9,1},{1... | collective-permute-start | bytes 393224 | tf_op jit(solution)/shard_map/ppermute | solution.py:77
  19.4 2.5 %collective-permute-start.8 = (f32[128,256]{1,0:T(8,128)S(1)}, f32[128,256]{1,0:T(8,128)S(1)}, u32[]{:S(2)}, u32[]{:S(2)}) collective-permute-start(f32[128,256]{1,0:T(8,128)S(1)} %add.5), channel_id=1, source_target_pairs={{0,2},{1,3},{2,11},{3,10},{4,6},{5,7},{6,15},{7,14},{8,1},{9,0},{1... | collective-permute-start | bytes 393224 | tf_op jit(solution)/shard_map/ppermute | solution.py:77
  21.8 1.9 %collective-permute-done.7 = f32[128,256]{1,0:T(8,128)S(1)} collective-permute-done((f32[128,256]{1,0:T(8,128)S(1)}, f32[128,256]{1,0:T(8,128)S(1)}, u32[]{:S(2)}, u32[]{:S(2)}) %collective-permute-start.7) | collective-permute-done | bytes 131104 | tf_op jit(solution)/shard_map/ppermute | solution.py:77
  23.7 2.1 %collective-permute-done.8 = f32[128,256]{1,0:T(8,128)S(1)} collective-permute-done((f32[128,256]{1,0:T(8,128)S(1)}, f32[128,256]{1,0:T(8,128)S(1)}, u32[]{:S(2)}, u32[]{:S(2)}) %collective-permute-start.8) | collective-permute-done | bytes 131104 | tf_op jit(solution)/shard_map/ppermute | solution.py:77
  25.8 0.0 copy-done.1
  25.8 0.7 %subtract_subtract_fusion = f32[128,256]{1,0:T(8,128)} fusion(f32[128,256]{1,0:T(8,128)S(1)} %collective-permute-done.8, f32[128,256]{1,0:T(8,128)S(1)} %copy-done.1, f32[128,256]{1,0:T(8,128)S(1)} %collective-permute-done.7), kind=kLoop, calls=%fused_computation.9 | loop fusion | flops 65536 | bytes 524288 | tf_op jit(solution)/shard_map/sub | solution.py:99
  (4 shorter events, 0.1 us)
Async XLA Ops:
  0.0 2.8 %collective-permute-start = (f32[256,256]{1,0:T(8,128)}, f32[256,256]{1,0:T(8,128)S(1)}, u32[]{:S(2)}, u32[]{:S(2)}) collective-permute-start(f32[256,256]{1,0:T(8,128)} %param.5), channel_id=1, source_target_pairs={{0,8},{1,9},{2,10},{3,11},{4,12},{5,13},{6,14},{7,15},{8,0},{9,1},... | collective-permute-start | bytes 786440 | tf_op jit(solution)/shard_map/ppermute | solution.py:77
  0.1 8.0 %collective-permute-start.3 = (f32[256,128]{1,0:T(8,128)}, f32[256,128]{1,0:T(8,128)S(1)}, u32[]{:S(2)}, u32[]{:S(2)}) collective-permute-start(f32[256,128]{1,0:T(8,128)} %bitcast.3), channel_id=1, source_target_pairs={{0,2},{1,3},{2,0},{3,1},{4,6},{5,7},{6,4},{7,5},{8,10},{9,11},{10,... | collective-permute-start | bytes 393224 | tf_op jit(solution)/shard_map/ppermute | solution.py:77
  2.8 11.9 %collective-permute-start.1 = (f32[256,256]{1,0:T(8,128)S(1)}, f32[256,256]{1,0:T(8,128)S(1)}, u32[]{:S(2)}, u32[]{:S(2)}) collective-permute-start(f32[256,256]{1,0:T(8,128)S(1)} %collective-permute-done), channel_id=1, source_target_pairs={{0,6},{1,7},{2,14},{3,15},{4,2},{5,3},{6,10},{7,11},{8,4},{9,5},{1... | collective-permute-start | bytes 786440 | tf_op jit(solution)/shard_map/ppermute | solution.py:77
  5.4 9.2 %collective-permute-start.2 = (f32[256,256]{1,0:T(8,128)S(1)}, f32[256,256]{1,0:T(8,128)S(1)}, u32[]{:S(2)}, u32[]{:S(2)}) collective-permute-start(f32[256,256]{1,0:T(8,128)S(1)} %collective-permute-done), channel_id=1, source_target_pairs={{0,2},{1,3},{2,10},{3,11},{4,6},{5,7},{6,14},{7,15},{8,0},{9,1},{1... | collective-permute-start | bytes 786440 | tf_op jit(solution)/shard_map/ppermute | solution.py:77
  6.9 5.0 %collective-permute-start.4 = (f32[256,128]{1,0:T(8,128)}, f32[256,128]{1,0:T(8,128)S(1)}, u32[]{:S(2)}, u32[]{:S(2)}) collective-permute-start(f32[256,128]{1,0:T(8,128)} %bitcast.4), channel_id=1, source_target_pairs={{0,16},{1,17},{2,18},{3,19},{4,20},{5,21},{6,22},{7,23},{8,24},{9,... | collective-permute-start | bytes 393224 | tf_op jit(solution)/shard_map/ppermute | solution.py:77
  8.1 6.6 %collective-permute-start.5 = (f32[256,128]{1,0:T(8,128)S(1)}, f32[256,128]{1,0:T(8,128)S(1)}, u32[]{:S(2)}, u32[]{:S(2)}) collective-permute-start(f32[256,128]{1,0:T(8,128)S(1)} %collective-permute-done.3), channel_id=1, source_target_pairs={{0,16},{1,17},{2,18},{3,19},{4,20},{5,21},{6,22},{7,23},{8,24},{9,... | collective-permute-start | bytes 393224 | tf_op jit(solution)/shard_map/ppermute | solution.py:77
  8.3 6.4 %copy-start = (f32[1,1,256,128]{3,2,1,0:T(8,128)S(1)}, f32[1,1,256,128]{3,2,1,0:T(8,128)}, u32[]{:S(2)}) copy-start(f32[1,1,256,128]{3,2,1,0:T(8,128)} %param.4) | copy-start | bytes 393220
  15.2 3.8 %collective-permute-start.6 = (f32[128,256]{1,0:T(8,128)S(1)}, f32[128,256]{1,0:T(8,128)S(1)}, u32[]{:S(2)}, u32[]{:S(2)}) collective-permute-start(f32[128,256]{1,0:T(8,128)S(1)} %fusion.1), channel_id=1, source_target_pairs={{0,8},{1,9},{2,10},{3,11},{4,12},{5,13},{6,14},{7,15},{8,0},{9,1},... | collective-permute-start | bytes 393224 | tf_op jit(solution)/shard_map/ppermute | solution.py:77
  18.4 7.5 %copy-start.1 = (f32[128,256]{1,0:T(8,128)S(1)}, f32[128,256]{1,0:T(8,128)}, u32[]{:S(2)}) copy-start(f32[128,256]{1,0:T(8,128)} %param.3) | copy-start | bytes 393220
  19.0 4.8 %collective-permute-start.7 = (f32[128,256]{1,0:T(8,128)S(1)}, f32[128,256]{1,0:T(8,128)S(1)}, u32[]{:S(2)}, u32[]{:S(2)}) collective-permute-start(f32[128,256]{1,0:T(8,128)S(1)} %add.5), channel_id=1, source_target_pairs={{0,3},{1,2},{2,10},{3,11},{4,7},{5,6},{6,14},{7,15},{8,0},{9,1},{1... | collective-permute-start | bytes 393224 | tf_op jit(solution)/shard_map/ppermute | solution.py:77
  19.4 6.5 %collective-permute-start.8 = (f32[128,256]{1,0:T(8,128)S(1)}, f32[128,256]{1,0:T(8,128)S(1)}, u32[]{:S(2)}, u32[]{:S(2)}) collective-permute-start(f32[128,256]{1,0:T(8,128)S(1)} %add.5), channel_id=1, source_target_pairs={{0,2},{1,3},{2,11},{3,10},{4,6},{5,7},{6,15},{7,14},{8,1},{9,0},{1... | collective-permute-start | bytes 393224 | tf_op jit(solution)/shard_map/ppermute | solution.py:77

commit v7 on v6

--- a/solution.py
+++ b/solution.py
@@ -96,7 +96,7 @@
     part = lax.optimization_barrier(mine) + theirs
     one = send(part, lambda r, c, l: (r, c ^ 1, 1 - l) if is_home(r, c) else (r ^ 1, c, l))
     two = send(part, lambda r, c, l: (r, c ^ 1, l) if is_home(r, c) else (r ^ 1, c, 1 - l))
-    return interface_panel - one - two
+    return interface_panel - two - one
 
 
 def solution(mesh):

time: 27.1 us -> 26.4 us (0.974); the launches traced: 26.5 us -> 26.3 us
  starting transfers between devices: 14 us -> 13 us
  waiting for transfers between devices: 10.9 us -> 11.6 us
    ppermute x9, starting transfers between devices: 14 us -> 13 us  [send(): return lax.ppermute(value, MESH_AXES, route(target))]
    ppermute x9, waiting for transfers between devices: 10.9 us -> 11.6 us  [send(): return lax.ppermute(value, MESH_AXES, route(target))]
where the time goes in v7:
time: 26.4 us; the launch traced here: 26.3 us
  starting transfers between devices  13 us (49%)
  waiting for transfers between devices  11.6 us (44%)
  matrix products  0.8 us (3%)
  other arithmetic  0.78 us (3%)
    ppermute x9, starting transfers between devices, send(): return lax.ppermute(value, MESH_AXES, route(target))  13 us
    ppermute x9, waiting for transfers between devices, send(): return lax.ppermute(value, MESH_AXES, route(target))  11.6 us
    dot_general x2, matrix products, multiply(): lax.dot_general(block, solved, (((0,), (0,)), ((), ())), precision=lax.Pr...  0.8 us
    sub x1, other arithmetic, pairs_of_planes(): return interface_panel - two - one  0.68 us
  transfers between devices with their start and end apart: 9, of which 5 were waited for; matrix products, arithmetic and copies ran while one was open for 2% of the time, Pallas kernels for 0%

profile of v7, /device:TPU:1, one launch (start us, length us, event | category | flops | bytes accessed | tf_op | source)
XLA Modules:
  0.0 26.3 jit_solution(16158213373604504204)
XLA Ops:
  0.0 0.1 collective-permute-start
  0.1 2.7 %collective-permute-start.3 = (f32[256,128]{1,0:T(8,128)}, f32[256,128]{1,0:T(8,128)S(1)}, u32[]{:S(2)}, u32[]{:S(2)}) collective-permute-start(f32[256,128]{1,0:T(8,128)} %bitcast.3), channel_id=1, source_target_pairs={{0,2},{1,3},{2,0},{3,1},{4,6},{5,7},{6,4},{7,5},{8,10},{9,11},{10,... | collective-permute-start | bytes 393224 | tf_op jit(solution)/shard_map/ppermute | solution.py:77
  2.8 0.0 collective-permute-done
  2.8 2.6 %collective-permute-start.1 = (f32[256,256]{1,0:T(8,128)S(1)}, f32[256,256]{1,0:T(8,128)S(1)}, u32[]{:S(2)}, u32[]{:S(2)}) collective-permute-start(f32[256,256]{1,0:T(8,128)S(1)} %collective-permute-done), channel_id=1, source_target_pairs={{0,6},{1,7},{2,14},{3,15},{4,2},{5,3},{6,10},{7,11},{8,4},{9,5},{1... | collective-permute-start | bytes 786440 | tf_op jit(solution)/shard_map/ppermute | solution.py:77
  5.4 1.4 %collective-permute-start.2 = (f32[256,256]{1,0:T(8,128)S(1)}, f32[256,256]{1,0:T(8,128)S(1)}, u32[]{:S(2)}, u32[]{:S(2)}) collective-permute-start(f32[256,256]{1,0:T(8,128)S(1)} %collective-permute-done), channel_id=1, source_target_pairs={{0,2},{1,3},{2,10},{3,11},{4,6},{5,7},{6,14},{7,15},{8,0},{9,1},{1... | collective-permute-start | bytes 786440 | tf_op jit(solution)/shard_map/ppermute | solution.py:77
  6.9 1.2 %collective-permute-start.4 = (f32[256,128]{1,0:T(8,128)}, f32[256,128]{1,0:T(8,128)S(1)}, u32[]{:S(2)}, u32[]{:S(2)}) collective-permute-start(f32[256,128]{1,0:T(8,128)} %bitcast.4), channel_id=1, source_target_pairs={{0,16},{1,17},{2,18},{3,19},{4,20},{5,21},{6,22},{7,23},{8,24},{9,... | collective-permute-start | bytes 393224 | tf_op jit(solution)/shard_map/ppermute | solution.py:77
  8.1 0.0 collective-permute-done.3
  8.1 0.3 collective-permute-start.5
  8.3 0.0 copy-start
  8.3 3.5 %collective-permute-done.4 = f32[256,128]{1,0:T(8,128)S(1)} collective-permute-done((f32[256,128]{1,0:T(8,128)}, f32[256,128]{1,0:T(8,128)S(1)}, u32[]{:S(2)}, u32[]{:S(2)}) %collective-permute-start.4) | collective-permute-done | bytes 131104 | tf_op jit(solution)/shard_map/ppermute | solution.py:77
  11.8 2.8 %collective-permute-done.5 = f32[256,128]{1,0:T(8,128)S(1)} collective-permute-done((f32[256,128]{1,0:T(8,128)S(1)}, f32[256,128]{1,0:T(8,128)S(1)}, u32[]{:S(2)}, u32[]{:S(2)}) %collective-permute-start.5) | collective-permute-done | bytes 131104 | tf_op jit(solution)/shard_map/ppermute | solution.py:77
  14.7 0.0 collective-permute-done.1
  14.7 0.0 collective-permute-done.2
  14.7 0.0 copy-done
  14.8 0.4 %fusion.1 = f32[128,256]{1,0:T(8,128)S(1)} fusion(f32[256,256]{1,0:T(8,128)S(1)} %get-tuple-element.22, f32[256,256]{1,0:T(8,128)S(1)} %get-tuple-element.21, f32[256,128]{1,0:T(8,128)S(1)} %get-tuple-element.25, f32[256,128]{1,0:T(8,128)S(1)} %get-tuple-element.24), kind=kOutput, calls=%fused_computation.2 | convolution fusion | flops 100859904 | bytes 917504 | tf_op jit(solution)/shard_map/dot_general | solution.py:10
  15.2 2.8 %collective-permute-start.6 = (f32[128,256]{1,0:T(8,128)S(1)}, f32[128,256]{1,0:T(8,128)S(1)}, u32[]{:S(2)}, u32[]{:S(2)}) collective-permute-start(f32[128,256]{1,0:T(8,128)S(1)} %fusion.1), channel_id=1, source_target_pairs={{0,8},{1,9},{2,10},{3,11},{4,12},{5,13},{6,14},{7,15},{8,0},{9,1},... | collective-permute-start | bytes 393224 | tf_op jit(solution)/shard_map/ppermute | solution.py:77
  18.0 0.4 %fusion = f32[128,256]{1,0:T(8,128)S(1)} fusion(f32[256,256]{1,0:T(8,128)S(1)} %get-tuple-element.22, f32[256,256]{1,0:T(8,128)S(1)} %get-tuple-element.21, f32[256,128]{1,0:T(8,128)S(1)} %broadcast_select_fusion.2, f32[256,128]{1,0:T(8,128)S(1)} %get-tuple-element.23), kind=kOutput, calls=%fused_computation.1 | convolution fusion | flops 100859904 | bytes 917504 | tf_op jit(solution)/shard_map/dot_general | solution.py:10
  18.4 0.0 copy-start.1
  18.4 0.6 %collective-permute-done.6 = f32[128,256]{1,0:T(8,128)S(1)} collective-permute-done((f32[128,256]{1,0:T(8,128)S(1)}, f32[128,256]{1,0:T(8,128)S(1)}, u32[]{:S(2)}, u32[]{:S(2)}) %collective-permute-start.6) | collective-permute-done | bytes 131104 | tf_op jit(solution)/shard_map/ppermute | solution.py:77
  19.0 1.9 %collective-permute-start.7 = (f32[128,256]{1,0:T(8,128)S(1)}, f32[128,256]{1,0:T(8,128)S(1)}, u32[]{:S(2)}, u32[]{:S(2)}) collective-permute-start(f32[128,256]{1,0:T(8,128)S(1)} %add.5), channel_id=1, source_target_pairs={{0,2},{1,3},{2,11},{3,10},{4,6},{5,7},{6,15},{7,14},{8,1},{9,0},{1... | collective-permute-start | bytes 393224 | tf_op jit(solution)/shard_map/ppermute | solution.py:77
  20.9 0.0 collective-permute-start.8
  20.9 3.3 %collective-permute-done.7 = f32[128,256]{1,0:T(8,128)S(1)} collective-permute-done((f32[128,256]{1,0:T(8,128)S(1)}, f32[128,256]{1,0:T(8,128)S(1)}, u32[]{:S(2)}, u32[]{:S(2)}) %collective-permute-start.7) | collective-permute-done | bytes 131104 | tf_op jit(solution)/shard_map/ppermute | solution.py:77
  24.2 1.4 %collective-permute-done.8 = f32[128,256]{1,0:T(8,128)S(1)} collective-permute-done((f32[128,256]{1,0:T(8,128)S(1)}, f32[128,256]{1,0:T(8,128)S(1)}, u32[]{:S(2)}, u32[]{:S(2)}) %collective-permute-start.8) | collective-permute-done | bytes 131104 | tf_op jit(solution)/shard_map/ppermute | solution.py:77
  25.6 0.0 copy-done.1
  25.6 0.7 %subtract_subtract_fusion = f32[128,256]{1,0:T(8,128)} fusion(f32[128,256]{1,0:T(8,128)S(1)} %collective-permute-done.8, f32[128,256]{1,0:T(8,128)S(1)} %copy-done.1, f32[128,256]{1,0:T(8,128)S(1)} %collective-permute-done.7), kind=kLoop, calls=%fused_computation.9 | loop fusion | flops 65536 | bytes 524288 | tf_op jit(solution)/shard_map/sub | solution.py:99
  (4 shorter events, 0.1 us)
Async XLA Ops:
  0.0 2.8 %collective-permute-start = (f32[256,256]{1,0:T(8,128)}, f32[256,256]{1,0:T(8,128)S(1)}, u32[]{:S(2)}, u32[]{:S(2)}) collective-permute-start(f32[256,256]{1,0:T(8,128)} %param.5), channel_id=1, source_target_pairs={{0,8},{1,9},{2,10},{3,11},{4,12},{5,13},{6,14},{7,15},{8,0},{9,1},... | collective-permute-start | bytes 786440 | tf_op jit(solution)/shard_map/ppermute | solution.py:77
  0.1 8.0 %collective-permute-start.3 = (f32[256,128]{1,0:T(8,128)}, f32[256,128]{1,0:T(8,128)S(1)}, u32[]{:S(2)}, u32[]{:S(2)}) collective-permute-start(f32[256,128]{1,0:T(8,128)} %bitcast.3), channel_id=1, source_target_pairs={{0,2},{1,3},{2,0},{3,1},{4,6},{5,7},{6,4},{7,5},{8,10},{9,11},{10,... | collective-permute-start | bytes 393224 | tf_op jit(solution)/shard_map/ppermute | solution.py:77
  2.8 11.9 %collective-permute-start.1 = (f32[256,256]{1,0:T(8,128)S(1)}, f32[256,256]{1,0:T(8,128)S(1)}, u32[]{:S(2)}, u32[]{:S(2)}) collective-permute-start(f32[256,256]{1,0:T(8,128)S(1)} %collective-permute-done), channel_id=1, source_target_pairs={{0,6},{1,7},{2,14},{3,15},{4,2},{5,3},{6,10},{7,11},{8,4},{9,5},{1... | collective-permute-start | bytes 786440 | tf_op jit(solution)/shard_map/ppermute | solution.py:77
  5.4 9.2 %collective-permute-start.2 = (f32[256,256]{1,0:T(8,128)S(1)}, f32[256,256]{1,0:T(8,128)S(1)}, u32[]{:S(2)}, u32[]{:S(2)}) collective-permute-start(f32[256,256]{1,0:T(8,128)S(1)} %collective-permute-done), channel_id=1, source_target_pairs={{0,2},{1,3},{2,10},{3,11},{4,6},{5,7},{6,14},{7,15},{8,0},{9,1},{1... | collective-permute-start | bytes 786440 | tf_op jit(solution)/shard_map/ppermute | solution.py:77
  6.9 5.0 %collective-permute-start.4 = (f32[256,128]{1,0:T(8,128)}, f32[256,128]{1,0:T(8,128)S(1)}, u32[]{:S(2)}, u32[]{:S(2)}) collective-permute-start(f32[256,128]{1,0:T(8,128)} %bitcast.4), channel_id=1, source_target_pairs={{0,16},{1,17},{2,18},{3,19},{4,20},{5,21},{6,22},{7,23},{8,24},{9,... | collective-permute-start | bytes 393224 | tf_op jit(solution)/shard_map/ppermute | solution.py:77
  8.1 6.6 %collective-permute-start.5 = (f32[256,128]{1,0:T(8,128)S(1)}, f32[256,128]{1,0:T(8,128)S(1)}, u32[]{:S(2)}, u32[]{:S(2)}) collective-permute-start(f32[256,128]{1,0:T(8,128)S(1)} %collective-permute-done.3), channel_id=1, source_target_pairs={{0,16},{1,17},{2,18},{3,19},{4,20},{5,21},{6,22},{7,23},{8,24},{9,... | collective-permute-start | bytes 393224 | tf_op jit(solution)/shard_map/ppermute | solution.py:77
  8.3 6.4 %copy-start = (f32[1,1,256,128]{3,2,1,0:T(8,128)S(1)}, f32[1,1,256,128]{3,2,1,0:T(8,128)}, u32[]{:S(2)}) copy-start(f32[1,1,256,128]{3,2,1,0:T(8,128)} %param.4) | copy-start | bytes 393220
  15.2 3.8 %collective-permute-start.6 = (f32[128,256]{1,0:T(8,128)S(1)}, f32[128,256]{1,0:T(8,128)S(1)}, u32[]{:S(2)}, u32[]{:S(2)}) collective-permute-start(f32[128,256]{1,0:T(8,128)S(1)} %fusion.1), channel_id=1, source_target_pairs={{0,8},{1,9},{2,10},{3,11},{4,12},{5,13},{6,14},{7,15},{8,0},{9,1},... | collective-permute-start | bytes 393224 | tf_op jit(solution)/shard_map/ppermute | solution.py:77
  18.4 7.2 %copy-start.1 = (f32[128,256]{1,0:T(8,128)S(1)}, f32[128,256]{1,0:T(8,128)}, u32[]{:S(2)}) copy-start(f32[128,256]{1,0:T(8,128)} %param.3) | copy-start | bytes 393220
  19.0 5.2 %collective-permute-start.7 = (f32[128,256]{1,0:T(8,128)S(1)}, f32[128,256]{1,0:T(8,128)S(1)}, u32[]{:S(2)}, u32[]{:S(2)}) collective-permute-start(f32[128,256]{1,0:T(8,128)S(1)} %add.5), channel_id=1, source_target_pairs={{0,2},{1,3},{2,11},{3,10},{4,6},{5,7},{6,15},{7,14},{8,1},{9,0},{1... | collective-permute-start | bytes 393224 | tf_op jit(solution)/shard_map/ppermute | solution.py:77
  20.9 4.7 %collective-permute-start.8 = (f32[128,256]{1,0:T(8,128)S(1)}, f32[128,256]{1,0:T(8,128)S(1)}, u32[]{:S(2)}, u32[]{:S(2)}) collective-permute-start(f32[128,256]{1,0:T(8,128)S(1)} %add.5), channel_id=1, source_target_pairs={{0,3},{1,2},{2,10},{3,11},{4,7},{5,6},{6,14},{7,15},{8,0},{9,1},{1... | collective-permute-start | bytes 393224 | tf_op jit(solution)/shard_map/ppermute | solution.py:77
